TPU v7x, 256 devices: a whole 4x4x8 slice. The times are simulated.
256 devices in a mesh: grp: 8 (over x, core), ctx: 32 (over z, y).
Axes of the slice: x: 4, y: 4, z: 8, core: 2. Of those that a mesh axis runs over, the one named last changes fastest.
Arguments:
- queries: bfloat16 [32768, 8192], P(('grp', 'ctx')), may hold values from -160 to 160
- key_tensor: bfloat16 [32768, 512], P(('grp', 'ctx')), may hold values from -5 to 5
- value_tensor: bfloat16 [32768, 512], P(('grp', 'ctx')), may hold values from -6 to 6
- out_grad: bfloat16 [32768, 8192], P(('grp', 'ctx')), may hold values from -6 to 6
- doc_lengths: int32 [682], replicated, may hold values from 1 to 192, 32768 in all
- placement: int32 [64], replicated, may hold values from 0 to 63, each once
Outputs:
- attended: bfloat16 [32768, 8192], P(('grp', 'ctx'))
- query_grad: bfloat16 [32768, 8192], P(('grp', 'ctx'))
- key_grad: bfloat16 [32768, 512], P(('grp', 'ctx'))
- value_grad: bfloat16 [32768, 512], P(('grp', 'ctx'))
Inputs may be any that keep to these rules, and one draw needn't show every extreme that they name: `doc_lengths`: the documents fill the window; one of them has exactly 192 tokens. `placement`: each block number appears once.
All inputs are finite; a program needn't handle non-finite values.
Results may differ from a plain program's by a relative error of at most 0.013.
Values may be sent and summed in bfloat16 or wider, within the bound.
No kernel may reach another device: no remote copies, remote signals or barrier semaphores. Data moves between devices by JAX's collectives and lax.ppermute only.
A program may use at most 128 MiB of HBM per device.

v0:
```python
import math

import jax
import jax.numpy as jnp
from jax import lax
from jax.sharding import PartitionSpec as P

QUERY_HEADS = 64
KEY_VALUE_HEADS = 4
HEAD_SIZE = 128
DOCUMENT_LIMIT = 192


def passed_along(shard, axis, by):
    length = lax.axis_size(axis)
    pairs = [(i, i + by) for i in range(length) if 0 <= i + by < length]
    return lax.ppermute(shard, axis, pairs)


def document_start(positions, doc_starts):
    return jnp.max(
        jnp.where(doc_starts[None, :] <= positions[:, None], doc_starts[None, :], 0), axis=1
    )


def attend(query_rows, key_rows, value_rows, gradient_rows, q_pos, k_pos, first_pos):
    row_total = query_rows.shape[0]
    span_length = key_rows.shape[0]
    group_width = QUERY_HEADS // KEY_VALUE_HEADS
    score_scale = 1.0 / math.sqrt(HEAD_SIZE)
    query_piece = query_rows.reshape(row_total, KEY_VALUE_HEADS, group_width, HEAD_SIZE)
    key_piece = key_rows.reshape(span_length, KEY_VALUE_HEADS, HEAD_SIZE)
    value_piece = value_rows.reshape(span_length, KEY_VALUE_HEADS, HEAD_SIZE)
    gradient_piece = gradient_rows.reshape(row_total, KEY_VALUE_HEADS, group_width, HEAD_SIZE)
    scores = (
        jnp.einsum("qhgd,whd->hgqw", query_piece, key_piece, preferred_element_type=jnp.float32)
        * score_scale
    )
    allowed = (k_pos[None, :] <= q_pos[:, None]) & (k_pos[None, :] >= first_pos[:, None])
    scores = jnp.where(allowed, scores, -1e30)
    row_top = jnp.max(scores, axis=-1, keepdims=True)
    weights_raw = jnp.where(allowed, jnp.exp(scores - row_top), 0.0)
    weights = weights_raw / jnp.sum(weights_raw, axis=-1, keepdims=True)
    weights_low = weights.astype(jnp.bfloat16)
    output = jnp.einsum(
        "hgqw,whd->qhgd", weights_low, value_piece, preferred_element_type=jnp.float32
    )
    output_lowered = output.astype(jnp.bfloat16)
    row_delta = jnp.sum(
        gradient_piece.astype(jnp.float32) * output_lowered.astype(jnp.float32), axis=-1
    )
    dprob = jnp.einsum(
        "qhgd,whd->hgqw", gradient_piece, value_piece, preferred_element_type=jnp.float32
    )
    dscore = weights * (dprob - jnp.transpose(row_delta, (1, 2, 0))[..., None]) * score_scale
    dscore = dscore.astype(jnp.bfloat16)
    query_gradient = jnp.einsum(
        "hgqw,whd->qhgd", dscore, key_piece, preferred_element_type=jnp.float32
    )
    key_gradient = jnp.einsum(
        "hgqw,qhgd->whd", dscore, query_piece, preferred_element_type=jnp.float32
    )
    value_gradient = jnp.einsum(
        "hgqw,qhgd->whd", weights_low, gradient_piece, preferred_element_type=jnp.float32
    )
    return (
        output_lowered.reshape(row_total, QUERY_HEADS * HEAD_SIZE),
        query_gradient.astype(jnp.bfloat16).reshape(row_total, QUERY_HEADS * HEAD_SIZE),
        key_gradient.reshape(span_length, KEY_VALUE_HEADS * HEAD_SIZE),
        value_gradient.reshape(span_length, KEY_VALUE_HEADS * HEAD_SIZE),
    )


def body(queries, key_tensor, value_tensor, out_grad, doc_lengths, placement):
    ctx_count = lax.axis_size("ctx")
    ctx_index = lax.axis_index("ctx")
    grp_index = lax.axis_index("grp")
    block_len = queries.shape[0] // 2
    slot_count = 2 * ctx_count
    group_tokens = block_len * slot_count
    columns = key_tensor.shape[1]
    span_length = DOCUMENT_LIMIT + block_len
    doc_ends = jnp.cumsum(doc_lengths)
    doc_starts = doc_ends - doc_lengths
    whole_k, whole_v = (
        lax.all_gather(key_tensor, "ctx", axis=0, tiled=True),
        lax.all_gather(value_tensor, "ctx", axis=0, tiled=True),
    )
    inverse = (
        jnp.zeros((slot_count,), jnp.int32)
        .at[placement]
        .set(jnp.arange(slot_count, dtype=jnp.int32))
    )
    order_k = whole_k.reshape(slot_count, block_len, columns)[inverse].reshape(
        group_tokens, columns
    )
    order_v = whole_v.reshape(slot_count, block_len, columns)[inverse].reshape(
        group_tokens, columns
    )
    prev_k, prev_v = passed_along(
        (order_k[group_tokens - DOCUMENT_LIMIT :], order_v[group_tokens - DOCUMENT_LIMIT :]),
        "grp",
        1,
    )
    buffer_k = jnp.concatenate([prev_k, order_k], axis=0)
    buffer_v = jnp.concatenate([prev_v, order_v], axis=0)
    group_base = grp_index * group_tokens
    dk_buffer = jnp.zeros((DOCUMENT_LIMIT + group_tokens, columns), jnp.float32)
    dv_buffer = jnp.zeros((DOCUMENT_LIMIT + group_tokens, columns), jnp.float32)
    out_pieces = []
    grad_pieces = []
    block_ids = []
    for half_index in range(2):
        block_id = lax.dynamic_index_in_dim(placement, 2 * ctx_index + half_index, keepdims=False)
        block_ids.append(block_id)
        local_start = block_id * block_len
        q_pos = group_base + local_start + jnp.arange(block_len, dtype=jnp.int32)
        k_pos = group_base + local_start - DOCUMENT_LIMIT + jnp.arange(span_length, dtype=jnp.int32)
        rows_slice = slice(half_index * block_len, (half_index + 1) * block_len)
        output_lowered, query_gradient, key_gradient, value_gradient = attend(
            queries[rows_slice],
            lax.dynamic_slice_in_dim(buffer_k, local_start, span_length, 0),
            lax.dynamic_slice_in_dim(buffer_v, local_start, span_length, 0),
            out_grad[rows_slice],
            q_pos,
            k_pos,
            document_start(q_pos, doc_starts),
        )
        out_pieces.append(output_lowered)
        grad_pieces.append(query_gradient)
        dk_buffer = lax.dynamic_update_slice_in_dim(
            dk_buffer,
            lax.dynamic_slice_in_dim(dk_buffer, local_start, span_length, 0) + key_gradient,
            local_start,
            0,
        )
        dv_buffer = lax.dynamic_update_slice_in_dim(
            dv_buffer,
            lax.dynamic_slice_in_dim(dv_buffer, local_start, span_length, 0) + value_gradient,
            local_start,
            0,
        )
    tail_k = dk_buffer[:DOCUMENT_LIMIT]
    tail_v = dv_buffer[:DOCUMENT_LIMIT]
    main_k = dk_buffer[DOCUMENT_LIMIT:]
    main_v = dv_buffer[DOCUMENT_LIMIT:]
    back_k, back_v = (
        passed_along(tail_k.astype(jnp.bfloat16), "grp", -1).astype(tail_k.dtype),
        passed_along(tail_v.astype(jnp.bfloat16), "grp", -1).astype(tail_v.dtype),
    )
    main_k = jnp.concatenate(
        [main_k[: group_tokens - DOCUMENT_LIMIT], main_k[group_tokens - DOCUMENT_LIMIT :] + back_k],
        axis=0,
    )
    main_v = jnp.concatenate(
        [main_v[: group_tokens - DOCUMENT_LIMIT], main_v[group_tokens - DOCUMENT_LIMIT :] + back_v],
        axis=0,
    )
    slot_k = main_k.reshape(slot_count, block_len, columns)[placement].reshape(
        group_tokens, columns
    )
    slot_v = main_v.reshape(slot_count, block_len, columns)[placement].reshape(
        group_tokens, columns
    )
    own_k, own_v = (
        lax.psum_scatter(slot_k, "ctx", scatter_dimension=0, tiled=True),
        lax.psum_scatter(slot_v, "ctx", scatter_dimension=0, tiled=True),
    )
    return (
        jnp.concatenate(out_pieces, axis=0),
        jnp.concatenate(grad_pieces, axis=0),
        own_k.astype(jnp.bfloat16),
        own_v.astype(jnp.bfloat16),
    )


def solution(mesh):
    in_specs = (
        P(("grp", "ctx"), None),
        P(("grp", "ctx"), None),
        P(("grp", "ctx"), None),
        P(("grp", "ctx"), None),
        P(),
        P(),
    )
    out_specs = (
        P(("grp", "ctx"), None),
        P(("grp", "ctx"), None),
        P(("grp", "ctx"), None),
        P(("grp", "ctx"), None),
    )
    return jax.shard_map(body, mesh=mesh, in_specs=in_specs, out_specs=out_specs, check_vma=False)
```

profile of v0, /device:TPU:1, one launch (start us, length us, event | category | flops | bytes accessed | tf_op | source)
XLA Modules:
  0.0 709.8 jit_solution(868230869199710322)
XLA Ops:
  7.2 0.7 all-gather.5.cloned.1.call-update
  7.9 0.7 all-gather.3.cloned.1.call-update
  8.7 1.3 fusion.46
  11.3 0.7 pad_bitcast_fusion
  12.4 1.8 slice_bitcast_fusion.3
  14.3 1.3 copy.124
  16.3 1.3 copy.130
  17.5 0.8 scatter_custom_fusion
  18.8 74.8 %all-gather.5.cloned.1.call-done = bf16[4096,512]{1,0:T(8,128)(2,1)} async-done(((bf16[128,512]{1,0:T(8,128)(2,1)}), bf16[4096,512]{1,0:T(8,128)(2,1)}) %all-gather.5.cloned.1.call-update) | async-done | bytes 4194320 | tf_op jit(solution)/shard_map/all_gather | solution.py:86
  93.6 5.0 gather_fusion.1
  98.6 76.8 %all-gather.3.cloned.1.call-done = bf16[4096,512]{1,0:T(8,128)(2,1)} async-done(((bf16[128,512]{1,0:T(8,128)(2,1)}), bf16[4096,512]{1,0:T(8,128)(2,1)}) %all-gather.3.cloned.1.call-update) | async-done | bytes 4194320 | tf_op jit(solution)/shard_map/all_gather | solution.py:87
  175.3 5.0 gather_fusion
  180.3 0.9 slice.85
  181.3 0.9 slice.86
  182.2 6.3 collective-permute-start.1
  188.5 1.9 collective-permute-start
  191.1 2.1 collective-permute-done
  193.2 1.7 fusion.37
  195.2 0.8 copy.72
  196.0 0.8 copy.66
  196.9 0.8 fusion.24
  197.7 2.2 fusion.47
  200.0 0.9 fusion.17
  201.2 2.1 multiply_reduce_fusion
  203.3 1.6 fusion.4
  204.9 2.3 fusion.22
  207.3 2.0 copy.91
  209.3 2.1 fusion.28
  211.4 2.2 fusion.48
  213.6 0.7 fusion.16
  214.4 1.3 copy-done
  215.7 2.0 multiply_reduce_fusion.1
  217.7 1.6 fusion.7
  219.3 2.3 fusion.26
  221.7 2.0 copy.89
  223.7 1.1 broadcast.53.clone
  225.0 2.1 collective-permute-start.2
  227.2 4.0 slice.87
  231.2 1.6 collective-permute-done.2
  232.8 7.5 %pad_maximum_fusion = f32[4096,512]{1,0:T(8,128)} fusion(f32[192,512]{1,0:T(8,128)S(1)} %slice_add_fusion.1, f32[3904,512]{1,0:T(8,128)} %slice.87), kind=kLoop, calls=%fused_computation.7 | loop fusion | flops 2097152 | bytes 16777216 | tf_op jit(solution)/shard_map/concatenate | solution.py:151
  240.3 7.7 %gather_fusion.2 = f32[64,64,512]{2,1,0:T(8,128)} fusion(f32[64,64,512]{2,1,0:T(8,128)} %bitcast.168, s32[1024]{0:T(1024)S(1)} %pad_clamp_fusion), kind=kCustom, calls=%fused_computation.2 | custom fusion | bytes 16777472 | tf_op jit(solution)/shard_map/gather | solution.py:159
  248.1 3.5 fusion.30
  251.6 1.2 copy.95
  252.8 3.1 fusion.33
  256.2 1.1 broadcast.53.clone.1
  257.5 2.2 collective-permute-start.3
  259.7 4.0 slice.90
  263.7 1.2 collective-permute-done.3
  264.9 7.5 %pad_maximum_fusion.1 = f32[4096,512]{1,0:T(8,128)} fusion(f32[192,512]{1,0:T(8,128)S(1)} %slice_add_fusion, f32[3904,512]{1,0:T(8,128)} %slice.90), kind=kLoop, calls=%fused_computation.8 | loop fusion | flops 2097152 | bytes 16777216 | tf_op jit(solution)/shard_map/concatenate | solution.py:155
  272.5 7.7 %gather_fusion.3 = f32[64,64,512]{2,1,0:T(8,128)} fusion(f32[64,64,512]{2,1,0:T(8,128)} %bitcast.167, s32[1024]{0:T(1024)S(1)} %pad_clamp_fusion), kind=kCustom, calls=%fused_computation.3 | custom fusion | bytes 16777472 | tf_op jit(solution)/shard_map/gather | solution.py:162
  280.2 1.6 copy-done.6
  281.8 0.7 fusion.21
  283.2 0.7 copy.154
  284.6 0.7 copy.156
  285.3 0.7 fusion.20
  286.7 0.7 copy.155
  287.4 0.7 copy.71
  288.1 0.7 copy.157
  288.8 1.5 pad_maximum_fusion.3
  290.3 1.5 pad_maximum_fusion.2
  291.8 178.0 %reduce-scatter.3.cloned.1.call-done = f32[128,512]{1,0:T(8,128)} async-done(((f32[4096,512]{1,0:T(8,128)}), f32[128,512]{1,0:T(8,128)}) %reduce-scatter.3.cloned.1.call-update) | async-done | bytes 262160 | tf_op jit(solution)/shard_map/reduce_scatter | solution.py:166
  469.8 1.6 convert_element_type.79
  471.4 230.2 %reduce-scatter.5.cloned.1.call-done = f32[128,512]{1,0:T(8,128)} async-done(((f32[4096,512]{1,0:T(8,128)}), f32[128,512]{1,0:T(8,128)}) %reduce-scatter.5.cloned.1.call-update) | async-done | bytes 262160 | tf_op jit(solution)/shard_map/reduce_scatter | solution.py:167
  701.6 1.6 convert_element_type.81
  (79 shorter events, 5.8 us)
Async XLA Ops:
  7.2 86.5 %all-gather.5.cloned.1.call-start = ((), (), s32[]{:S(2)}) async-start(), calls=%async_computation.3 | async-start | bytes 4325376 | tf_op jit(solution)/shard_map/all_gather | solution.py:86
  7.9 167.4 %all-gather.3.cloned.1.call-start = ((), (), s32[]{:S(2)}) async-start(), calls=%async_computation.2 | async-start | bytes 4325376 | tf_op jit(solution)/shard_map/all_gather | solution.py:87
  8.6 461.2 %reduce-scatter.3.cloned.1.call-start = ((), (), s32[]{:S(2)}) async-start(), calls=%async_computation.4 | async-start | bytes 8650752 | tf_op jit(solution)/shard_map/reduce_scatter | solution.py:166
  12.4 3.4 copy-start.13
  15.8 181.1 %copy-start.3 = (bf16[8,8,64,128]{3,2,1,0:T(8,128)(2,1)}, bf16[8,8,64,128]{3,2,1,0:T(8,128)(2,1)S(1)}, u32[]{:S(2)}) copy-start(bf16[8,8,64,128]{3,2,1,0:T(8,128)(2,1)S(1)} %copy.126) | copy-start | bytes 3145732
  15.8 1.7 copy-start.19
  15.8 2.8 copy-start.18
  182.2 8.9 %collective-permute-start.1 = (bf16[192,512]{1,0:T(8,128)(2,1)S(1)}, bf16[192,512]{1,0:T(8,128)(2,1)S(1)}, u32[]{:S(2)}, u32[]{:S(2)}) collective-permute-start(bf16[192,512]{1,0:T(8,128)(2,1)S(1)} %bitcast.204), channel_id=1, source_target_pairs={{0,32},{32,64},{64,96},{96,128},{128,160},{160,192},{192,224},{1,3... | collective-permute-start | bytes 589832 | tf_op jit(solution)/shard_map/ppermute | solution.py:17
  188.5 4.7 collective-permute-start
  195.2 4.8 copy-start.11
  200.0 1.2 copy-start.1
  200.0 1.3 copy-start.17
  203.3 1.6 copy-start.4
  204.9 2.3 copy-start.5
  213.6 2.1 copy-start.16
  214.4 1.3 copy-start
  217.7 1.6 copy-start.2
  219.3 2.3 copy-start.7
  223.7 1.1 copy-start.15
  223.7 1.2 copy-start.14
  225.0 7.7 %collective-permute-start.2 = (bf16[192,512]{1,0:T(8,128)(2,1)S(1)}, bf16[192,512]{1,0:T(8,128)(2,1)S(1)}, u32[]{:S(2)}, u32[]{:S(2)}) collective-permute-start(bf16[192,512]{1,0:T(8,128)(2,1)S(1)} %slice.104), channel_id=1, source_target_pairs={{32,0},{64,32},{96,64},{128,96},{160,128},{192,160},{224,192},{33,... | collective-permute-start | bytes 589832 | tf_op jit(solution)/shard_map/ppermute | solution.py:17
  248.0 453.6 %reduce-scatter.5.cloned.1.call-start = ((), (), s32[]{:S(2)}) async-start(), calls=%async_computation.5 | async-start | bytes 8650752 | tf_op jit(solution)/shard_map/reduce_scatter | solution.py:167
  257.5 7.4 %collective-permute-start.3 = (bf16[192,512]{1,0:T(8,128)(2,1)S(1)}, bf16[192,512]{1,0:T(8,128)(2,1)S(1)}, u32[]{:S(2)}, u32[]{:S(2)}) collective-permute-start(bf16[192,512]{1,0:T(8,128)(2,1)S(1)} %slice.103), channel_id=1, source_target_pairs={{32,0},{64,32},{96,64},{128,96},{160,128},{192,160},{224,192},{33,... | collective-permute-start | bytes 589832 | tf_op jit(solution)/shard_map/ppermute | solution.py:17
  280.2 1.6 copy-start.6
  280.2 1.6 copy-start.12
  281.8 2.1 copy-start.9
  282.5 2.8 copy-start.8
  285.3 2.1 copy-start.10
Sparse Core Ops, SparseCore 0:
  10.6 82.9 all-gather.4
  96.2 79.0 all-gather.2
  248.1 221.6 reduce-scatter.2
  474.2 227.3 reduce-scatter.4
where the time goes:
time: 714 us; the launch traced here: 710 us
  waiting for transfers between devices  567 us (79%)
  local copies, waits for them, and re-layouts  61.9 us (9%)
  other arithmetic  30.1 us (4%)
  matrix products  22.9 us (3%)
  between operations  15.7 us (2%)
  starting transfers between devices  12.7 us (2%)
    reduce_scatter x1, waiting for transfers between devices, body(): lax.psum_scatter(slot_v, 'ctx', scatter_dimension=0, tiled=True)  230 us
    reduce_scatter x1, waiting for transfers between devices, body(): lax.psum_scatter(slot_k, 'ctx', scatter_dimension=0, tiled=True)  178 us
    all_gather x1, waiting for transfers between devices, body(): lax.all_gather(value_tensor, 'ctx', axis=0, tiled=True)  76.8 us
    all_gather x1, waiting for transfers between devices, body(): lax.all_gather(key_tensor, 'ctx', axis=0, tiled=True)  74.8 us
  transfers between devices with their start and end apart: 8, of which 8 were waited for; matrix products, arithmetic and copies ran while one was open for 8% of the time, Pallas kernels for 0%

commit v1 on v0

v1 whole, which is shorter than its diff:
```python
import functools
import math

import jax
import jax.numpy as jnp
from jax import lax
from jax.experimental import pallas as pl
from jax.experimental.pallas import tpu as pltpu
from jax.sharding import PartitionSpec as P

KV_HEADS = 4
GROUP_WIDTH = 16
HEAD = 128
LIMIT = 192
BLOCK = 64
SLOTS = 64
BEFORE = LIMIT // BLOCK
ROWS = 16
PARTS = BLOCK // ROWS
PIECES = 2 * KV_HEADS * PARTS
CHUNK = 4
SCALE = 1.0 / math.sqrt(HEAD)
LOG2E = math.log2(math.e)

VMEM = pl.BlockSpec(memory_space=pltpu.VMEM)
SMEM = pl.BlockSpec(memory_space=pltpu.SMEM)


def pack_kernel(k_ref, v_ref, out_ref):
    for tensor, ref in enumerate((k_ref, v_ref)):
        for head in range(KV_HEADS):
            for part in range(PARTS):
                piece = (tensor * KV_HEADS + head) * PARTS + part
                for half in range(2):
                    out_ref[piece, half] = ref[
                        pl.ds(half * BLOCK + part * ROWS, ROWS), pl.ds(head * HEAD, HEAD)
                    ]


def last_kernel(place_ref, pieces_ref, out_ref):
    def one(slot, carry):
        block = place_ref[slot]

        @pl.when(block >= SLOTS - BEFORE)
        def _():
            out_ref[block - (SLOTS - BEFORE)] = pieces_ref[slot]

        return carry

    lax.fori_loop(0, SLOTS, one, 0)


def spread_kernel(place_ref, pieces_ref, prev_ref, out_ref, ordered):
    ordered[:BEFORE] = prev_ref[...]

    def put(slot, carry):
        ordered[place_ref[slot] + BEFORE] = pieces_ref[slot]
        return carry

    lax.fori_loop(0, SLOTS, put, 0, unroll=8)

    def take(slot, carry):
        block = place_ref[slot]
        for back in range(BEFORE):
            out_ref[slot, back] = ordered[block + back]
        return carry

    lax.fori_loop(0, SLOTS, take, 0, unroll=8)


def head_kernel(place_ref, parts_ref, out_ref, total):
    total[...] = jnp.zeros_like(total)

    def one(slot, carry):
        block = place_ref[slot]

        @pl.when(block < BEFORE)
        def _():
            for back in range(BEFORE):
                total[block + back] += parts_ref[slot, back].astype(jnp.float32)

        return carry

    lax.fori_loop(0, SLOTS, one, 0)
    out_ref[...] = total[:BEFORE].astype(jnp.bfloat16)


def sum_kernel(place_ref, parts_ref, next_ref, out_ref, total):
    total[...] = jnp.zeros_like(total)
    total[SLOTS:] = next_ref[...].astype(jnp.float32)

    def add(slot, carry):
        block = place_ref[slot]
        for back in range(BEFORE):
            total[block + back] += parts_ref[slot, back].astype(jnp.float32)
        return carry

    lax.fori_loop(0, SLOTS, add, 0, unroll=4)

    def take(slot, carry):
        out_ref[slot] = total[place_ref[slot] + BEFORE].astype(jnp.bfloat16)
        return carry

    lax.fori_loop(0, SLOTS, take, 0, unroll=8)


def finish_kernel(pieces_ref, dk_ref, dv_ref, out_k_ref, out_v_ref):
    for tensor, (own, out) in enumerate(((dk_ref, out_k_ref), (dv_ref, out_v_ref))):
        for head in range(KV_HEADS):
            for part in range(PARTS):
                piece = (tensor * KV_HEADS + head) * PARTS + part
                for half in range(2):
                    place = (
                        pl.ds(half * BLOCK + part * ROWS, ROWS),
                        pl.ds(head * HEAD, HEAD),
                    )
                    out[place] = (
                        own[place] + pieces_ref[piece, half].astype(jnp.float32)
                    ).astype(jnp.bfloat16)


def attend_kernel(
    low_ref, q_ref, g_ref, k_ref, v_ref, far_ref,
    att_ref, dq_ref, far_grad_ref, dk_ref, dv_ref, bias_ref,
):
    half = pl.program_id(0)
    head = pl.program_id(1)
    span = LIMIT + BLOCK
    lanes = CHUNK * BLOCK

    @pl.when(head == 0)
    def _():
        key_index = lax.broadcasted_iota(jnp.int32, (span, lanes), 0)
        query_index = lax.broadcasted_iota(jnp.int32, (span, lanes), 1) % BLOCK
        allowed = (key_index <= query_index + LIMIT) & (key_index >= low_ref[0])
        bias_ref[...] = jnp.where(allowed, 0.0, -1e30)

    def keys_of(tensor, own_ref):
        far = [
            far_ref[tensor, head, part, half, back]
            for back in range(BEFORE)
            for part in range(PARTS)
        ]
        return jnp.concatenate(far + [own_ref[...]], axis=0)

    keys = keys_of(0, k_ref)
    values = keys_of(1, v_ref)
    keys_t = keys.T
    values_t = values.T

    def rows_of(ref, first):
        return jnp.concatenate(
            [ref[:, pl.ds((first + i) * HEAD, HEAD)] for i in range(CHUNK)], axis=0
        )

    def put(ref, first, cols):
        rows = cols.T.astype(jnp.bfloat16)
        for i in range(CHUNK):
            ref[:, pl.ds((first + i) * HEAD, HEAD)] = rows[i * BLOCK : (i + 1) * BLOCK]

    nt = (((1,), (1,)), ((), ()))
    nn = (((1,), (0,)), ((), ()))
    dot = functools.partial(lax.dot_general, preferred_element_type=jnp.float32)
    key_grad = jnp.zeros((span, HEAD), jnp.float32)
    value_grad = jnp.zeros((span, HEAD), jnp.float32)
    for first in range(0, GROUP_WIDTH, CHUNK):
        query = rows_of(q_ref, first)
        grad = rows_of(g_ref, first)
        scores = dot(keys, query, nt) * (SCALE * LOG2E) + bias_ref[...]
        dprob = dot(values, grad, nt)
        raw = jnp.exp2(scores - jnp.max(scores, axis=0, keepdims=True))
        weights = raw * (1.0 / jnp.sum(raw, axis=0, keepdims=True))
        weights_low = weights.astype(jnp.bfloat16)
        out_t = dot(values_t, weights_low, nn)
        put(att_ref, first, out_t)
        delta = jnp.sum(weights * dprob, axis=0, keepdims=True)
        dscore = (weights * (dprob - delta)).astype(jnp.bfloat16)
        put(dq_ref, first, dot(keys_t, dscore, nn) * SCALE)
        key_grad += dot(dscore, query, nn)
        value_grad += dot(weights_low, grad, nn)
    key_grad *= SCALE
    for tensor, grads, own in ((0, key_grad, dk_ref), (1, value_grad, dv_ref)):
        low = grads[:LIMIT].astype(jnp.bfloat16)
        for back in range(BEFORE):
            for part in range(PARTS):
                row = back * BLOCK + part * ROWS
                far_grad_ref[tensor, head, part, half, back] = low[row : row + ROWS]
        own[...] = grads[LIMIT:]


def attend(low, queries, key_tensor, value_tensor, out_grad, far):
    span = LIMIT + BLOCK
    wide = pl.BlockSpec((BLOCK, GROUP_WIDTH * HEAD), lambda j, h: (j, h))
    narrow = pl.BlockSpec((BLOCK, HEAD), lambda j, h: (j, h))
    return pl.pallas_call(
        attend_kernel,
        grid=(2, KV_HEADS),
        in_specs=[
            pl.BlockSpec((1, 1, CHUNK * BLOCK), lambda j, h: (j, 0, 0)),
            wide, wide, narrow, narrow, VMEM,
        ],
        out_specs=[wide, wide, VMEM, narrow, narrow],
        out_shape=[
            jax.ShapeDtypeStruct(queries.shape, jnp.bfloat16),
            jax.ShapeDtypeStruct(queries.shape, jnp.bfloat16),
            jax.ShapeDtypeStruct(far.shape, jnp.bfloat16),
            jax.ShapeDtypeStruct(key_tensor.shape, jnp.float32),
            jax.ShapeDtypeStruct(value_tensor.shape, jnp.float32),
        ],
        scratch_shapes=[pltpu.VMEM((span, CHUNK * BLOCK), jnp.float32)],
        compiler_params=pltpu.CompilerParams(
            dimension_semantics=("arbitrary", "arbitrary"),
            vmem_limit_bytes=40 * 1024 * 1024,
        ),
    )(low, queries, out_grad, key_tensor, value_tensor, far)


def call(kernel, outs, specs, *args, scratch=()):
    return pl.pallas_call(
        kernel,
        in_specs=specs,
        out_specs=[VMEM] * len(outs),
        out_shape=outs,
        scratch_shapes=scratch,
        compiler_params=pltpu.CompilerParams(vmem_limit_bytes=16 * 1024 * 1024),
    )(*args)


def body(queries, key_tensor, value_tensor, out_grad, doc_lengths, placement):
    ctx_count = lax.axis_size("ctx")
    grp_count = lax.axis_size("grp")
    ctx_index = lax.axis_index("ctx")
    grp_index = lax.axis_index("grp")
    tile = (ROWS, HEAD)
    bf16 = functools.partial(jax.ShapeDtypeStruct, dtype=jnp.bfloat16)
    exchange = functools.partial(
        lax.all_to_all, axis_name="ctx", split_axis=0, concat_axis=0, tiled=True
    )

    (packed,) = call(
        pack_kernel, [bf16((PIECES, 2, *tile))], [VMEM, VMEM], key_tensor, value_tensor
    )
    pieces = exchange(packed).reshape(SLOTS, *tile)
    (last,) = call(last_kernel, [bf16((BEFORE, *tile))], [SMEM, VMEM], placement, pieces)
    prev = lax.ppermute(last, "grp", [(i, i + 1) for i in range(grp_count - 1)])
    (wanted,) = call(
        spread_kernel,
        [bf16((SLOTS, BEFORE, *tile))],
        [SMEM, VMEM, VMEM],
        placement,
        pieces,
        prev,
        scratch=[pltpu.VMEM((SLOTS + BEFORE, *tile), jnp.bfloat16)],
    )
    far = exchange(wanted.reshape(ctx_count, 2, BEFORE, *tile))

    doc_ends = jnp.cumsum(doc_lengths)
    doc_starts = doc_ends - doc_lengths
    blocks = lax.dynamic_slice_in_dim(placement, 2 * ctx_index, 2)
    start = (grp_index * SLOTS + blocks) * BLOCK
    q_pos = (start[:, None] + jnp.arange(BLOCK, dtype=jnp.int32)).reshape(-1)
    first = jnp.max(
        jnp.where(doc_starts[None, :] <= q_pos[:, None], doc_starts[None, :], 0), axis=1
    )
    low = first.reshape(2, BLOCK) - (start - LIMIT)[:, None]
    low = jnp.tile(low, (1, CHUNK)).reshape(2, 1, CHUNK * BLOCK)

    attended, query_grad, far_grad, own_k, own_v = attend(
        low, queries, key_tensor, value_tensor, out_grad,
        far.reshape(2, KV_HEADS, PARTS, 2, BEFORE, *tile),
    )

    parts = exchange(far_grad.reshape(ctx_count, 2, BEFORE, *tile))
    parts = parts.reshape(SLOTS, BEFORE, *tile)
    (ahead,) = call(
        head_kernel,
        [bf16((BEFORE, *tile))],
        [SMEM, VMEM],
        placement,
        parts,
        scratch=[pltpu.VMEM((2 * BEFORE, *tile), jnp.float32)],
    )
    behind = lax.ppermute(ahead, "grp", [(i + 1, i) for i in range(grp_count - 1)])
    (sums,) = call(
        sum_kernel,
        [bf16((SLOTS, *tile))],
        [SMEM, VMEM, VMEM],
        placement,
        parts,
        behind,
        scratch=[pltpu.VMEM((SLOTS + BEFORE, *tile), jnp.float32)],
    )
    sums = exchange(sums.reshape(ctx_count, 2, *tile))
    key_grad, value_grad = call(
        finish_kernel,
        [bf16(key_tensor.shape), bf16(value_tensor.shape)],
        [VMEM] * 3,
        sums,
        own_k,
        own_v,
    )
    return attended, query_grad, key_grad, value_grad


def solution(mesh):
    rows = P(("grp", "ctx"), None)
    return jax.shard_map(
        body,
        mesh=mesh,
        in_specs=(rows, rows, rows, rows, P(), P()),
        out_specs=(rows, rows, rows, rows),
        check_vma=False,
    )
```

time: 714 us -> 134 us (0.19)
  waiting for transfers between devices: 567 us -> 24.6 us
  blocking collectives: 0 us -> 67.4 us
  local copies, waits for them, and re-layouts: 61.9 us -> 4.51 us
  other arithmetic: 30.1 us -> 0.79 us
  matrix products: 22.9 us -> 0 us
  Pallas kernels: 0 us -> 22.9 us
  between operations: 15.7 us -> 0.73 us
    reduce_scatter x2 -> x0, waiting for transfers between devices: 408 us -> none  [the longest x1 230 us: body(): lax.psum_scatter(slot_v, 'ctx', scatter_dimension=0, tiled=True)]
    all_gather x2 -> x0, waiting for transfers between devices: 152 us -> none  [the longest x1 76.8 us: body(): lax.all_gather(value_tensor, 'ctx', axis=0, tiled=True)]
    all_to_all x0 -> x3, blocking collectives: none -> 67.4 us  [the longest x1 27.1 us: body(): parts = exchange(far_grad.reshape(ctx_count, 2, BEFORE, *tile))]
    gather x4 -> x0, local copies, waits for them, and re-layouts: 25.3 us -> none  [the longest x1 7.71 us: body(): main_v.reshape(slot_count, block_len, columns)[placement]]
    dot_general x12 -> x0, matrix products: 22.9 us -> none  [the longest x2 6.62 us: attend(): jnp.einsum('hgqw,qhgd->whd', weights_low, gradient_piece, preferred_eleme...]
    pallas_call x0 -> x7, Pallas kernels: none -> 22.9 us  [the longest x1 16.6 us: attend(): pl.pallas_call(attend_kernel, grid=(2, KV_HEADS), in_specs=[pl.BlockSpec(...]
    all_to_all x0 -> x1, waiting for transfers between devices: none -> 20.9 us  [body(): far = exchange(wanted.reshape(ctx_count, 2, BEFORE, *tile))]
    concatenate x5 -> x0, other arithmetic: 19.6 us -> none  [the longest x1 7.51 us: body(): jnp.concatenate([main_v[:group_tokens - DOCUMENT_LIMIT], main_v[group_tok...]
  transfers between devices with their start and end apart: 8 -> 3, of which waited for: 8 -> 3; matrix products, arithmetic and copies ran while one was open for 8% -> 1% of each run, Pallas kernels for 0% -> 0%
where the time goes in v1:
time: 134 us; the launch traced here: 133 us
  blocking collectives  67.4 us (50%)
  waiting for transfers between devices  24.6 us (18%)
  Pallas kernels  22.9 us (17%)
  starting transfers between devices  12.3 us (9%)
  local copies, waits for them, and re-layouts  4.51 us (3%)
    all_to_all x1, blocking collectives, body(): parts = exchange(far_grad.reshape(ctx_count, 2, BEFORE, *tile))  27.1 us
    all_to_all x1, blocking collectives, body(): pieces = exchange(packed).reshape(SLOTS, *tile)  23.2 us
    all_to_all x1, waiting for transfers between devices, body(): far = exchange(wanted.reshape(ctx_count, 2, BEFORE, *tile))  20.9 us
    all_to_all x1, blocking collectives, body(): sums = exchange(sums.reshape(ctx_count, 2, *tile))  17.2 us
    pallas_call x1, Pallas kernels, attend(): pl.pallas_call(attend_kernel, grid=(2, KV_HEADS), in_specs=[pl.BlockSpec(...  16.6 us
    pallas_call x6, Pallas kernels, call(): pl.pallas_call(kernel, in_specs=specs, out_specs=[VMEM] * len(outs), out_...  6.23 us
    ppermute x1, starting transfers between devices, body(): prev = lax.ppermute(last, 'grp', [(i, i + 1) for i in range(grp_count - 1)])  5.46 us
    unnamed x18, local copies, waits for them, and re-layouts  4.06 us
  transfers between devices with their start and end apart: 3, of which 3 were waited for; matrix products, arithmetic and copies ran while one was open for 1% of the time, Pallas kernels for 0%

profile of v1, /device:TPU:1, one launch (start us, length us, event | category | flops | bytes accessed | tf_op | source)
XLA Modules:
  0.0 133.1 jit_solution(14902880230833740887)
XLA Ops:
  0.6 0.0 copy-start.2
  0.6 0.9 copy-done.2
  1.5 0.0 copy-start.4
  1.5 0.9 copy-done.4
  2.4 0.0 copy-start
  2.4 0.0 copy-start.3
  2.4 0.0 copy-start.5
  2.5 23.2 %all_to_all.20 = bf16[32,2,16,128]{3,2,1,0:T(8,128)(2,1)S(1)} all-to-all(bf16[32,2,16,128]{3,2,1,0:T(8,128)(2,1)S(1)} %shard_map.93), channel_id=1, replica_groups=mesh['grp'=8,'ctx'=32] {'ctx'}, dimensions={0} | all-to-all | bytes 524288 | tf_op jit(solution)/shard_map/all_to_all | solution.py:243
  25.7 0.0 copy-start.6
  25.7 0.7 copy-done.6
  26.3 0.0 copy-start.7
  26.3 0.0 copy-start.8
  26.3 1.4 %shard_map.94 = bf16[3,16,128]{2,1,0:T(8,128)(2,1)S(1)} custom-call(s32[64]{0:T(128)S(1)} %copy-done.6, bf16[64,16,128]{2,1,0:T(8,128)(2,1)S(1)} %bitcast.13), custom_call_target="tpu_custom_call" | custom-call | tf_op jit(solution)/shard_map/pallas_call | solution.py:219
  27.7 5.5 %collective-permute-start = (bf16[3,16,128]{2,1,0:T(8,128)(2,1)S(1)}, bf16[3,16,128]{2,1,0:T(8,128)(2,1)S(1)}, u32[]{:S(2)}, u32[]{:S(2)}) collective-permute-start(bf16[3,16,128]{2,1,0:T(8,128)(2,1)S(1)} %shard_map.94), channel_id=1, source_target_pairs={{0,32},{32,64},{64,96},{96,128},{128,160},{160,192},{192,224},{1,3... | collective-permute-start | bytes 36872 | tf_op jit(solution)/shard_map/ppermute | solution.py:245
  33.2 0.8 collective-permute-done.prev_ref
  34.0 1.6 %shard_map.95 = bf16[64,3,16,128]{3,2,1,0:T(8,128)(2,1)} custom-call(s32[64]{0:T(128)S(1)} %copy-done.6, bf16[64,16,128]{2,1,0:T(8,128)(2,1)S(1)} %bitcast.14, bf16[3,16,128]{2,1,0:T(8,128)(2,1)S(1)} %collective-permute-done.prev_ref), custom_call_target="tpu_custom_call" | custom-call | tf_op jit(solution)/shard_map/pallas_call | solution.py:219
  35.6 3.9 %all-to-all-start.1 = ((bf16[32,2,3,16,128]{4,3,2,1,0:T(8,128)(2,1)}), bf16[32,2,3,16,128]{4,3,2,1,0:T(8,128)(2,1)S(1)}, u32[]{:S(2)}, u32[]{:S(2)}) async-start(bf16[32,2,3,16,128]{4,3,2,1,0:T(8,128)(2,1)} %bitcast.3), calls=%async_computation.1 | async-start | bytes 1572864 | tf_op jit(solution)/shard_map/all_to_all | solution.py:255
  39.6 0.0 copy-done.7
  39.6 0.1 broadcast_add_fusion
  39.7 0.1 iota_add_fusion
  39.7 0.1 add.38
  39.8 0.0 copy-done.8
  39.8 0.3 reduce-window.9
  40.1 0.1 slice.10
  40.2 0.1 slice_reduce_fusion
  40.3 0.1 add_bitcast_fusion
  40.4 0.2 select_reduce_fusion
  40.6 0.1 reshape.82
  40.7 0.1 broadcast_subtract_fusion
  40.8 0.1 tile.9.low_ref
  40.8 20.9 %all-to-all-done.1 = bf16[32,2,3,16,128]{4,3,2,1,0:T(8,128)(2,1)S(1)} async-done(((bf16[32,2,3,16,128]{4,3,2,1,0:T(8,128)(2,1)}), bf16[32,2,3,16,128]{4,3,2,1,0:T(8,128)(2,1)S(1)}, u32[]{:S(2)}, u32[]{:S(2)}) %all-to-all-start.1) | async-done | bytes 786464 | tf_op jit(solution)/shard_map/all_to_all | solution.py:255
  61.7 0.0 copy-done
  61.7 0.0 copy-done.3
  61.7 0.0 copy-done.5
  61.7 0.0 copy-start.1
  61.7 1.6 %copy-done.1 = bf16[128,8192]{1,0:T(8,128)(2,1)S(1)} copy-done((bf16[128,8192]{1,0:T(8,128)(2,1)S(1)}, bf16[128,8192]{1,0:T(8,128)(2,1)}, u32[]{:S(2)}) %copy-start.1) | copy-done | bytes 2097176
  63.3 16.6 %shard_map.96 = (bf16[128,8192]{1,0:T(8,128)(2,1)}, bf16[128,8192]{1,0:T(8,128)(2,1)}, bf16[2,4,4,2,3,16,128]{6,5,4,3,2,1,0:T(8,128)(2,1)S(1)}, f32[128,512]{1,0:T(8,128)S(1)}, f32[128,512]{1,0:T(8,128)S(1)}) custom-call(s32[2,1,256]{2,1,0:T(1,128)S(1)} %tile.9.low_ref, bf16[128,8192]{1,0:T(8,128)(2,1)S(1)} %copy-done, bf16[128,8192]{1,0:T(8,128)(2,1)S(1)} %copy-done.1, ...), custom_call_target="tpu_custom_call" | custom-call | tf_op jit(solution)/shard_map/pallas_call | solution.py:195
  79.9 27.1 %all_to_all.21 = bf16[32,2,3,16,128]{4,3,2,1,0:T(8,128)(2,1)S(1)} all-to-all(bf16[32,2,3,16,128]{4,3,2,1,0:T(8,128)(2,1)S(1)} %bitcast.16), channel_id=1, replica_groups=mesh['grp'=8,'ctx'=32] {'ctx'}, dimensions={0} | all-to-all | bytes 1572864 | tf_op jit(solution)/shard_map/all_to_all | solution.py:273
  107.0 1.4 %shard_map.97 = bf16[3,16,128]{2,1,0:T(8,128)(2,1)S(1)} custom-call(s32[64]{0:T(128)S(1)} %copy-done.7, bf16[64,3,16,128]{3,2,1,0:T(8,128)(2,1)S(1)} %bitcast.10), custom_call_target="tpu_custom_call" | custom-call | tf_op jit(solution)/shard_map/pallas_call | solution.py:219
  108.5 2.9 %collective-permute-start.1 = (bf16[3,16,128]{2,1,0:T(8,128)(2,1)S(1)}, bf16[3,16,128]{2,1,0:T(8,128)(2,1)S(1)}, u32[]{:S(2)}, u32[]{:S(2)}) collective-permute-start(bf16[3,16,128]{2,1,0:T(8,128)(2,1)S(1)} %shard_map.97), channel_id=1, source_target_pairs={{32,0},{64,32},{96,64},{128,96},{160,128},{192,160},{224,192},{33,... | collective-permute-start | bytes 36872 | tf_op jit(solution)/shard_map/ppermute | solution.py:283
  111.4 2.9 %collective-permute-done.1.next_ref = bf16[3,16,128]{2,1,0:T(8,128)(2,1)S(1)} collective-permute-done((bf16[3,16,128]{2,1,0:T(8,128)(2,1)S(1)}, bf16[3,16,128]{2,1,0:T(8,128)(2,1)S(1)}, u32[]{:S(2)}, u32[]{:S(2)}) %collective-permute-start.1) | collective-permute-done | bytes 12320 | tf_op jit(solution)/shard_map/ppermute | solution.py:283
  114.3 1.0 shard_map.98
  115.2 17.2 %all_to_all.22.pieces_ref = bf16[32,2,16,128]{3,2,1,0:T(8,128)(2,1)S(1)} all-to-all(bf16[32,2,16,128]{3,2,1,0:T(8,128)(2,1)S(1)} %bitcast.15), channel_id=1, replica_groups=mesh['grp'=8,'ctx'=32] {'ctx'}, dimensions={0} | all-to-all | bytes 524288 | tf_op jit(solution)/shard_map/all_to_all | solution.py:293
  132.4 0.7 shard_map.99
  (5 shorter events, 0.1 us)
Async XLA Ops:
  0.6 0.9 copy-start.2
  1.5 0.9 copy-start.4
  2.4 59.3 %copy-start = (bf16[128,8192]{1,0:T(8,128)(2,1)S(1)}, bf16[128,8192]{1,0:T(8,128)(2,1)}, u32[]{:S(2)}) copy-start(bf16[128,8192]{1,0:T(8,128)(2,1)} %q_ref.1) | copy-start | bytes 6291460
  2.4 59.3 %copy-start.3 = (bf16[128,512]{1,0:T(8,128)(2,1)S(1)}, bf16[128,512]{1,0:T(8,128)(2,1)}, u32[]{:S(2)}) copy-start(bf16[128,512]{1,0:T(8,128)(2,1)} %k_ref.3) | copy-start | bytes 393220
  2.4 59.3 %copy-start.5 = (bf16[128,512]{1,0:T(8,128)(2,1)S(1)}, bf16[128,512]{1,0:T(8,128)(2,1)}, u32[]{:S(2)}) copy-start(bf16[128,512]{1,0:T(8,128)(2,1)} %v_ref.3) | copy-start | bytes 393220
  25.7 0.7 copy-start.6
  26.3 13.3 %copy-start.7 = (s32[64]{0:T(128)S(1)}, s32[64]{0:T(128)}, u32[]{:S(2)}) copy-start(s32[64]{0:T(128)} %place_ref.7) | copy-start | bytes 772
  26.3 13.5 %copy-start.8 = (s32[682]{0:T(1024)S(1)}, s32[682]{0:T(1024)}, u32[]{:S(2)}) copy-start(s32[682]{0:T(1024)} %param.10) | copy-start | bytes 8188
  27.7 6.3 %collective-permute-start = (bf16[3,16,128]{2,1,0:T(8,128)(2,1)S(1)}, bf16[3,16,128]{2,1,0:T(8,128)(2,1)S(1)}, u32[]{:S(2)}, u32[]{:S(2)}) collective-permute-start(bf16[3,16,128]{2,1,0:T(8,128)(2,1)S(1)} %shard_map.94), channel_id=1, source_target_pairs={{0,32},{32,64},{64,96},{96,128},{128,160},{160,192},{192,224},{1,3... | collective-permute-start | bytes 36872 | tf_op jit(solution)/shard_map/ppermute | solution.py:245
  35.6 26.1 %all-to-all-start.1 = ((bf16[32,2,3,16,128]{4,3,2,1,0:T(8,128)(2,1)}), bf16[32,2,3,16,128]{4,3,2,1,0:T(8,128)(2,1)S(1)}, u32[]{:S(2)}, u32[]{:S(2)}) async-start(bf16[32,2,3,16,128]{4,3,2,1,0:T(8,128)(2,1)} %bitcast.3), calls=%async_computation.1 | async-start | bytes 1572864 | tf_op jit(solution)/shard_map/all_to_all | solution.py:255
  61.7 1.6 %copy-start.1 = (bf16[128,8192]{1,0:T(8,128)(2,1)S(1)}, bf16[128,8192]{1,0:T(8,128)(2,1)}, u32[]{:S(2)}) copy-start(bf16[128,8192]{1,0:T(8,128)(2,1)} %g_ref.1) | copy-start | bytes 6291460
  108.5 5.8 %collective-permute-start.1 = (bf16[3,16,128]{2,1,0:T(8,128)(2,1)S(1)}, bf16[3,16,128]{2,1,0:T(8,128)(2,1)S(1)}, u32[]{:S(2)}, u32[]{:S(2)}) collective-permute-start(bf16[3,16,128]{2,1,0:T(8,128)(2,1)S(1)} %shard_map.97), channel_id=1, source_target_pairs={{32,0},{64,32},{96,64},{128,96},{160,128},{192,160},{224,192},{33,... | collective-permute-start | bytes 36872 | tf_op jit(solution)/shard_map/ppermute | solution.py:283

commit v2 on v1

v2 whole, which is shorter than its diff:
```python
import functools
import math

import jax
import jax.numpy as jnp
from jax import lax
from jax.experimental import pallas as pl
from jax.experimental.pallas import tpu as pltpu
from jax.sharding import PartitionSpec as P

KV_HEADS = 4
GROUP_WIDTH = 16
HEAD = 128
LIMIT = 192
BLOCK = 64
SLOTS = 64
BEFORE = LIMIT // BLOCK
ROWS = 16
PARTS = BLOCK // ROWS
PIECES = 2 * KV_HEADS * PARTS
CHUNK = 4
SCALE = 1.0 / math.sqrt(HEAD)
LOG2E = math.log2(math.e)
MIB = 1024 * 1024

VMEM = pl.BlockSpec(memory_space=pltpu.VMEM)
SMEM = pl.BlockSpec(memory_space=pltpu.SMEM)
ANY = pl.BlockSpec(memory_space=pltpu.HBM)


def pack_kernel(rows_ref, out_ref):
    for tensor in range(2):
        for head in range(KV_HEADS):
            for part in range(PARTS):
                piece = (tensor * KV_HEADS + head) * PARTS + part
                for half in range(2):
                    out_ref[piece, half] = rows_ref[
                        tensor,
                        pl.ds(half * BLOCK + part * ROWS, ROWS),
                        pl.ds(head * HEAD, HEAD),
                    ]


def order_kernel(place_ref, pieces_ref, ordered_ref, last_ref):
    for slot in range(SLOTS):
        ordered_ref[place_ref[slot]] = pieces_ref[slot]
    last_ref[...] = ordered_ref[SLOTS - BEFORE :]


def spread_kernel(place_ref, ordered_ref, prev_ref, out_ref, done_ref, whole):
    whole[:BEFORE] = prev_ref[...]
    whole[BEFORE:] = ordered_ref[...]
    done_ref[...] = jnp.zeros_like(done_ref)
    for slot in range(SLOTS):
        out_ref[slot] = whole[pl.ds(place_ref[slot], BEFORE)]


def slots_of(place_ref, slot_of):
    for slot in range(SLOTS):
        slot_of[place_ref[slot]] = slot


def part_sum(slot_of, parts_ref, block):
    return sum(
        parts_ref[slot_of[block + ahead], BEFORE - ahead].astype(jnp.float32)
        for ahead in range(1, BEFORE + 1)
        if 0 <= block + ahead < SLOTS
    )


def head_kernel(place_ref, parts_ref, after_ref, out_ref, slot_of):
    slots_of(place_ref, slot_of)
    for back in range(BEFORE):
        out_ref[back] = part_sum(slot_of, parts_ref, back - BEFORE).astype(jnp.bfloat16)


def sum_kernel(place_ref, parts_ref, sums_ref, tail_ref, slot_of):
    slots_of(place_ref, slot_of)
    for block in range(SLOTS - 1):
        total = part_sum(slot_of, parts_ref, block)
        sums_ref[slot_of[block]] = total.astype(jnp.bfloat16)
        if block >= SLOTS - BEFORE:
            tail_ref[block - (SLOTS - BEFORE)] = total
    tail_ref[BEFORE - 1] = jnp.zeros((ROWS, HEAD), jnp.float32)


def tail_kernel(place_ref, sums_ref, tail_ref, next_ref, out_ref, slot_of):
    out_ref[...] = sums_ref[...]
    slots_of(place_ref, slot_of)
    for tail in range(BEFORE):
        total = tail_ref[tail] + next_ref[tail].astype(jnp.float32)
        out_ref[slot_of[SLOTS - BEFORE + tail]] = total.astype(jnp.bfloat16)


def finish_kernel(pieces_ref, dk_ref, dv_ref, out_k_ref, out_v_ref):
    for tensor, (own, out) in enumerate(((dk_ref, out_k_ref), (dv_ref, out_v_ref))):
        for head in range(KV_HEADS):
            for part in range(PARTS):
                piece = (tensor * KV_HEADS + head) * PARTS + part
                for half in range(2):
                    place = (
                        pl.ds(half * BLOCK + part * ROWS, ROWS),
                        pl.ds(head * HEAD, HEAD),
                    )
                    out[place] = (
                        own[place] + pieces_ref[piece, half].astype(jnp.float32)
                    ).astype(jnp.bfloat16)


def rows_of(ref, first, width=CHUNK):
    return jnp.concatenate(
        [ref[:, pl.ds((first + i) * HEAD, HEAD)] for i in range(width)], axis=0
    )


NT = (((1,), (1,)), ((), ()))
NN = (((1,), (0,)), ((), ()))
dot = functools.partial(lax.dot_general, preferred_element_type=jnp.float32)


def mask_to(bias_ref, low_ref, first_key):
    keys, lanes = bias_ref.shape
    key_index = first_key + lax.broadcasted_iota(jnp.int32, (keys, lanes), 0)
    query_index = lax.broadcasted_iota(jnp.int32, (keys, lanes), 1) % BLOCK
    allowed = (key_index <= query_index + LIMIT) & (key_index >= low_ref[0])
    bias_ref[...] = jnp.where(allowed, 0.0, -1e30)


def far_rows(far_ref, tensor, head, half):
    return [
        far_ref[tensor, head, part, half, back]
        for back in range(BEFORE)
        for part in range(PARTS)
    ]


def own_kernel(
    low_ref, q_ref, g_ref, k_ref, v_ref, after_ref, stat_ref, bias_ref
):
    key_index = LIMIT + lax.broadcasted_iota(jnp.int32, bias_ref.shape[1:], 0)
    query_index = lax.broadcasted_iota(jnp.int32, bias_ref.shape[1:], 1) % BLOCK
    for half in range(2):
        allowed = (key_index <= query_index + LIMIT) & (key_index >= low_ref[half])
        bias_ref[half] = jnp.where(allowed, 0.0, -1e30)

    for half in range(2):
        rows = pl.ds(half * BLOCK, BLOCK)
        for head in range(KV_HEADS):
            cols = pl.ds(head * HEAD, HEAD)
            for first in range(0, GROUP_WIDTH, CHUNK):
                lanes = pl.ds(first * BLOCK, CHUNK * BLOCK)
                query = rows_of(q_ref.at[rows], head * GROUP_WIDTH + first)
                grad = rows_of(g_ref.at[rows], head * GROUP_WIDTH + first)
                scores = dot(k_ref[rows, cols], query, NT) * (SCALE * LOG2E) + bias_ref[half]
                dprob = dot(v_ref[rows, cols], grad, NT)
                top = jnp.max(scores, axis=0, keepdims=True)
                raw = jnp.exp2(scores - top)
                stat_ref[half, head, 0:1, lanes] = top
                stat_ref[half, head, 1:2, lanes] = jnp.sum(raw, axis=0, keepdims=True)
                stat_ref[half, head, 2:3, lanes] = jnp.sum(raw * dprob, axis=0, keepdims=True)


def far_kernel(
    low_ref, q_ref, g_ref, stat_ref, far_ref, far_grad_ref, low_out_ref,
    bias_ref, q_rows, g_rows, sems,
):
    steps = [(half, head) for half in range(2) for head in range(KV_HEADS)]
    cuts = (0, 1, 4, 8)
    loads = {}
    for i, (first, last) in enumerate(zip(cuts[:-1], cuts[1:])):
        half, head = steps[first]
        place = (
            pl.ds(half * BLOCK, BLOCK),
            pl.ds(head * GROUP_WIDTH * HEAD, (last - first) * GROUP_WIDTH * HEAD),
        )
        loads[first] = [
            pltpu.make_async_copy(ref.at[place], rows.at[place], sems.at[i, j])
            for j, (ref, rows) in enumerate(((q_ref, q_rows), (g_ref, g_rows)))
        ]
        for load in loads[first]:
            load.start()
    low_out_ref[...] = low_ref[...]
    lanes = GROUP_WIDTH * BLOCK
    key_index = lax.broadcasted_iota(jnp.int32, (LIMIT, CHUNK * BLOCK), 0)
    for half in range(2):
        bias = jnp.where(key_index >= low_ref[half], 0.0, -1e30)
        bias_ref[half] = jnp.concatenate([bias] * (GROUP_WIDTH // CHUNK), axis=1)

    for step, (half, head) in enumerate(steps):
        rows = pl.ds(half * BLOCK, BLOCK)
        for load in loads.get(step, ()):
            load.wait()
        first = head * GROUP_WIDTH
        keys = jnp.concatenate(far_rows(far_ref, 0, head, half), axis=0)
        values = jnp.concatenate(far_rows(far_ref, 1, head, half), axis=0)
        query = rows_of(q_rows.at[rows], first, GROUP_WIDTH)
        grad = rows_of(g_rows.at[rows], first, GROUP_WIDTH)
        scores = dot(keys, query, NT) * (SCALE * LOG2E) + bias_ref[half]
        dprob = dot(values, grad, NT)
        own_top, own_total, own_delta = [
            stat_ref[half, head, i : i + 1, :lanes] for i in range(3)
        ]
        top = jnp.maximum(own_top, jnp.max(scores, axis=0, keepdims=True))
        raw = jnp.exp2(scores - top)
        fade = jnp.exp2(own_top - top)
        total = own_total * fade + jnp.sum(raw, axis=0, keepdims=True)
        delta = own_delta * fade + jnp.sum(raw * dprob, axis=0, keepdims=True)
        share = 1.0 / total
        weights = raw * share
        dscore = (weights * (dprob - delta * share)).astype(jnp.bfloat16)
        key_grad = dot(dscore, query, NN) * SCALE
        value_grad = dot(weights.astype(jnp.bfloat16), grad, NN)
        for tensor, grads in ((0, key_grad), (1, value_grad)):
            rounded = grads.astype(jnp.bfloat16)
            for back in range(BEFORE):
                for part in range(PARTS):
                    row = back * BLOCK + part * ROWS
                    far_grad_ref[tensor, head, part, half, back] = rounded[row : row + ROWS]


def rest_kernel(
    low_ref, q_ref, g_ref, k_ref, v_ref, far_ref, att_ref, dq_ref, dk_ref, dv_ref, bias_ref
):
    half = pl.program_id(0)
    head = pl.program_id(1)

    @pl.when(head == 0)
    def _():
        mask_to(bias_ref, low_ref, 0)

    keys = jnp.concatenate(far_rows(far_ref, 0, head, half) + [k_ref[...]], axis=0)
    values = jnp.concatenate(far_rows(far_ref, 1, head, half) + [v_ref[...]], axis=0)
    keys_t = keys.T
    values_t = values.T

    def put(ref, first, cols):
        rows = cols.T.astype(jnp.bfloat16)
        for i in range(CHUNK):
            ref[:, pl.ds((first + i) * HEAD, HEAD)] = rows[i * BLOCK : (i + 1) * BLOCK]

    key_grad = jnp.zeros((BLOCK, HEAD), jnp.float32)
    value_grad = jnp.zeros((BLOCK, HEAD), jnp.float32)
    for first in range(0, GROUP_WIDTH, CHUNK):
        query = rows_of(q_ref, first)
        grad = rows_of(g_ref, first)
        scores = dot(keys, query, NT) * (SCALE * LOG2E) + bias_ref[...]
        dprob = dot(values, grad, NT)
        raw = jnp.exp2(scores - jnp.max(scores, axis=0, keepdims=True))
        weights = raw * (1.0 / jnp.sum(raw, axis=0, keepdims=True))
        weights_low = weights.astype(jnp.bfloat16)
        put(att_ref, first, dot(values_t, weights_low, NN))
        delta = jnp.sum(weights * dprob, axis=0, keepdims=True)
        dscore = (weights * (dprob - delta)).astype(jnp.bfloat16)
        put(dq_ref, first, dot(keys_t, dscore, NN) * SCALE)
        key_grad += dot(dscore[LIMIT:], query, NN)
        value_grad += dot(weights_low[LIMIT:], grad, NN)
    dk_ref[...] = key_grad * SCALE
    dv_ref[...] = value_grad


LOW = pl.BlockSpec((1, 1, CHUNK * BLOCK), lambda j, h: (j, 0, 0))
WIDE = pl.BlockSpec((BLOCK, GROUP_WIDTH * HEAD), lambda j, h: (j, h))
NARROW = pl.BlockSpec((BLOCK, HEAD), lambda j, h: (j, h))
STAT = pl.BlockSpec((1, 1, 8, GROUP_WIDTH * BLOCK), lambda j, h: (j, h, 0, 0))


def grid_call(kernel, keys, in_specs, out_specs, out_shape, *args):
    return pl.pallas_call(
        kernel,
        grid=(2, KV_HEADS),
        in_specs=in_specs,
        out_specs=out_specs,
        out_shape=out_shape,
        scratch_shapes=[pltpu.VMEM((keys, CHUNK * BLOCK), jnp.float32)],
        compiler_params=pltpu.CompilerParams(
            dimension_semantics=("arbitrary", "arbitrary"),
            vmem_limit_bytes=24 * MIB,
        ),
    )(*args)


def attend_own(low, queries, out_grad, key_tensor, value_tensor, after):
    return call(
        own_kernel,
        [jax.ShapeDtypeStruct((2, KV_HEADS, 8, GROUP_WIDTH * BLOCK), jnp.float32)],
        [VMEM] * 5 + [ANY],
        low, queries, out_grad, key_tensor, value_tensor, after,
        scratch=[pltpu.VMEM((2, BLOCK, CHUNK * BLOCK), jnp.float32)],
        limit=24 * MIB,
    )


def attend_far(low, queries, out_grad, stat, far):
    return call(
        far_kernel,
        [
            jax.ShapeDtypeStruct(far.shape, jnp.bfloat16),
            jax.ShapeDtypeStruct(low.shape, jnp.int32),
        ],
        [VMEM, ANY, ANY, VMEM, VMEM],
        low, queries, out_grad, stat, far,
        scratch=[
            pltpu.VMEM((2, LIMIT, GROUP_WIDTH * BLOCK), jnp.float32),
            pltpu.VMEM(queries.shape, jnp.bfloat16),
            pltpu.VMEM(queries.shape, jnp.bfloat16),
            pltpu.SemaphoreType.DMA((3, 2)),
        ],
        limit=52 * MIB,
    )


def attend_rest(low, queries, out_grad, key_tensor, value_tensor, far):
    wide = jax.ShapeDtypeStruct(queries.shape, jnp.bfloat16)
    narrow = jax.ShapeDtypeStruct(key_tensor.shape, jnp.float32)
    return grid_call(
        rest_kernel, LIMIT + BLOCK, [LOW, WIDE, WIDE, NARROW, NARROW, VMEM],
        [WIDE, WIDE, NARROW, NARROW], [wide, wide, narrow, narrow],
        low, queries, out_grad, key_tensor, value_tensor, far,
    )


def call(kernel, outs, specs, *args, out_specs=None, scratch=(), limit=8 * MIB):
    return pl.pallas_call(
        kernel,
        in_specs=specs,
        out_specs=out_specs or [VMEM] * len(outs),
        out_shape=outs,
        scratch_shapes=scratch,
        compiler_params=pltpu.CompilerParams(vmem_limit_bytes=limit),
    )(*args)


def body(queries, key_tensor, value_tensor, out_grad, doc_lengths, placement):
    ctx_count = lax.axis_size("ctx")
    grp_count = lax.axis_size("grp")
    ctx_index = lax.axis_index("ctx")
    grp_index = lax.axis_index("grp")
    tile = (ROWS, HEAD)
    bf16 = functools.partial(jax.ShapeDtypeStruct, dtype=jnp.bfloat16)
    exchange = functools.partial(
        lax.all_to_all, axis_name="ctx", split_axis=0, concat_axis=0, tiled=True
    )

    doc_ends = jnp.cumsum(doc_lengths)
    doc_starts = doc_ends - doc_lengths
    blocks = lax.dynamic_slice_in_dim(placement, 2 * ctx_index, 2)
    start = (grp_index * SLOTS + blocks) * BLOCK
    q_pos = (start[:, None] + jnp.arange(BLOCK, dtype=jnp.int32)).reshape(-1)
    first = jnp.max(
        jnp.where(doc_starts[None, :] <= q_pos[:, None], doc_starts[None, :], 0), axis=1
    )
    low = first.reshape(2, BLOCK) - (start - LIMIT)[:, None]
    low = jnp.tile(low, (1, CHUNK)).reshape(2, 1, CHUNK * BLOCK)

    (packed,) = call(
        pack_kernel,
        [bf16((PIECES, 2, *tile))],
        [VMEM],
        jnp.stack([key_tensor, value_tensor]),
    )
    place = jnp.clip(placement, 0, SLOTS - 1)
    pieces = exchange(packed).reshape(SLOTS, *tile)
    ordered, last = call(
        order_kernel,
        [bf16((SLOTS, *tile)), bf16((BEFORE, *tile))],
        [SMEM, VMEM],
        place,
        pieces,
    )
    prev = lax.ppermute(last, "grp", [(i, i + 1) for i in range(grp_count - 1)])
    wanted, done = call(
        spread_kernel,
        [bf16((SLOTS, BEFORE, *tile)), jax.ShapeDtypeStruct((8, HEAD), jnp.float32)],
        [SMEM, VMEM, VMEM],
        place,
        ordered,
        prev,
        scratch=[pltpu.VMEM((SLOTS + BEFORE, *tile), jnp.bfloat16)],
    )
    far = exchange(wanted.reshape(ctx_count, 2, BEFORE, *tile))
    far = far.reshape(2, KV_HEADS, PARTS, 2, BEFORE, *tile)
    (stat,) = attend_own(low, queries, out_grad, key_tensor, value_tensor, done)
    far_grad, low = attend_far(low, queries, out_grad, stat, far)
    attended, query_grad, own_k, own_v = attend_rest(
        low, queries, out_grad, key_tensor, value_tensor, far
    )

    parts = exchange(far_grad.reshape(ctx_count, 2, BEFORE, *tile))
    parts = parts.reshape(SLOTS, BEFORE, *tile)
    slot_of = pltpu.SMEM((SLOTS,), jnp.int32)
    (ahead,) = call(
        head_kernel,
        [bf16((BEFORE, *tile))],
        [SMEM, VMEM, ANY],
        place,
        parts,
        own_k,
        scratch=[slot_of],
    )
    behind = lax.ppermute(ahead, "grp", [(i + 1, i) for i in range(grp_count - 1)])
    sums, tail = call(
        sum_kernel,
        [bf16((SLOTS, *tile)), jax.ShapeDtypeStruct((BEFORE, *tile), jnp.float32)],
        [SMEM, VMEM],
        place,
        parts,
        scratch=[slot_of],
    )
    (sums,) = call(
        tail_kernel,
        [bf16((SLOTS, *tile))],
        [SMEM, VMEM, VMEM, VMEM],
        place,
        sums,
        tail,
        behind,
        scratch=[slot_of],
    )
    sums = exchange(sums.reshape(ctx_count, 2, *tile))
    key_grad, value_grad = call(
        finish_kernel,
        [bf16(key_tensor.shape), bf16(value_tensor.shape)],
        [VMEM] * 3,
        sums,
        own_k,
        own_v,
    )
    return attended, query_grad, key_grad, value_grad


def solution(mesh):
    rows = P(("grp", "ctx"), None)
    return jax.shard_map(
        body,
        mesh=mesh,
        in_specs=(rows, rows, rows, rows, P(), P()),
        out_specs=(rows, rows, rows, rows),
        check_vma=False,
    )
```

time: 134 us -> 122 us (0.910)
  blocking collectives: 67.4 us -> 17 us
  starting transfers between devices: 12.3 us -> 29.2 us
  waiting for transfers between devices: 24.6 us -> 34.9 us
  Pallas kernels: 22.9 us -> 30.2 us
  other arithmetic: 0.79 us -> 2.6 us
  local copies, waits for them, and re-layouts: 4.51 us -> 6.16 us
    all_to_all x2 -> x0, blocking collectives: 50.2 us -> none  [the longest x1 27.1 us: body(): parts = exchange(far_grad.reshape(ctx_count, 2, BEFORE, *tile))]
    all_to_all x0 -> x2, starting transfers between devices: none -> 16.9 us  [the longest x1 12 us: body(): pieces = exchange(packed).reshape(SLOTS, *tile)]
    all_to_all x0 -> x2, waiting for transfers between devices: none -> 15 us  [the longest x1 10.5 us: body(): pieces = exchange(packed).reshape(SLOTS, *tile)]
    pallas_call x7 -> x10, Pallas kernels: 22.9 us -> 30.2 us  [the longest x1 15.8 us: grid_call(): pl.pallas_call(kernel, grid=(2, KV_HEADS), in_specs=in_specs, out_specs=o...]
    all_to_all x1, waiting for transfers between devices: 20.9 us -> 17.6 us  [body(): far = exchange(wanted.reshape(ctx_count, 2, BEFORE, *tile))]
    unnamed x18 -> x24, local copies, waits for them, and re-layouts: 4.06 us -> 5.71 us
  transfers between devices with their start and end apart: 3 -> 5, of which waited for: 3 -> 5; matrix products, arithmetic and copies ran while one was open for 1% -> 2% of each run, Pallas kernels for 0% -> 15%
where the time goes in v2:
time: 122 us; the launch traced here: 121 us
  waiting for transfers between devices  34.9 us (29%)
  Pallas kernels  30.2 us (25%)
  starting transfers between devices  29.2 us (24%)
  blocking collectives  17 us (14%)
  local copies, waits for them, and re-layouts  6.16 us (5%)
  other arithmetic  2.6 us (2%)
    all_to_all x1, waiting for transfers between devices, body(): far = exchange(wanted.reshape(ctx_count, 2, BEFORE, *tile))  17.6 us
    all_to_all x1, blocking collectives, body(): sums = exchange(sums.reshape(ctx_count, 2, *tile))  17 us
    pallas_call x1, Pallas kernels, grid_call(): pl.pallas_call(kernel, grid=(2, KV_HEADS), in_specs=in_specs, out_specs=o...  15.8 us
    pallas_call x9, Pallas kernels, call(): pl.pallas_call(kernel, in_specs=specs, out_specs=out_specs or [VMEM] * le...  14.4 us
    all_to_all x1, starting transfers between devices, body(): pieces = exchange(packed).reshape(SLOTS, *tile)  12 us
    all_to_all x1, waiting for transfers between devices, body(): pieces = exchange(packed).reshape(SLOTS, *tile)  10.5 us
    unnamed x24, local copies, waits for them, and re-layouts  5.71 us
    ppermute x1, starting transfers between devices, body(): prev = lax.ppermute(last, 'grp', [(i, i + 1) for i in range(grp_count - 1)])  5.46 us
  transfers between devices with their start and end apart: 5, of which 5 were waited for; matrix products, arithmetic and copies ran while one was open for 2% of the time, Pallas kernels for 15%

profile of v2, /device:TPU:1, one launch (start us, length us, event | category | flops | bytes accessed | tf_op | source)
XLA Modules:
  0.0 120.9 jit_solution(2508363527386341998)
XLA Ops:
  0.6 0.0 copy-start.4
  0.6 0.0 copy-start.5
  0.7 0.0 copy-start.11
  0.7 0.0 copy-start.10
  0.7 0.0 copy-start
  0.7 1.1 pad_maximum_fusion.rows_ref
  1.8 0.7 shard_map.93
  2.6 12.0 %all-to-all-start = ((bf16[32,2,16,128]{3,2,1,0:T(8,128)(2,1)}), bf16[32,2,16,128]{3,2,1,0:T(8,128)(2,1)S(1)}, u32[]{:S(2)}, u32[]{:S(2)}) async-start(bf16[32,2,16,128]{3,2,1,0:T(8,128)(2,1)} %shard_map.93), calls=%async_computation | async-start | bytes 524288 | tf_op jit(solution)/shard_map/all_to_all | solution.py:362
  14.6 0.7 broadcast_clamp_fusion.place_ref
  15.3 10.5 %all-to-all-done = bf16[32,2,16,128]{3,2,1,0:T(8,128)(2,1)S(1)} async-done(((bf16[32,2,16,128]{3,2,1,0:T(8,128)(2,1)}), bf16[32,2,16,128]{3,2,1,0:T(8,128)(2,1)S(1)}, u32[]{:S(2)}, u32[]{:S(2)}) %all-to-all-start) | async-done | bytes 262176 | tf_op jit(solution)/shard_map/all_to_all | solution.py:362
  25.8 0.6 shard_map.94
  26.4 5.5 %collective-permute-start = (bf16[3,16,128]{2,1,0:T(8,128)(2,1)S(1)}, bf16[3,16,128]{2,1,0:T(8,128)(2,1)S(1)}, u32[]{:S(2)}, u32[]{:S(2)}) collective-permute-start(bf16[3,16,128]{2,1,0:T(8,128)(2,1)S(1)} %get-tuple-element.19), channel_id=1, source_target_pairs={{0,32},{32,64},{64,96},{96,128},{128,160},{160,192},{192,224},{1,3... | collective-permute-start | bytes 36872 | tf_op jit(solution)/shard_map/ppermute | solution.py:370
  31.9 0.8 collective-permute-done.prev_ref
  32.7 0.6 shard_map.95
  33.3 0.0 copy-start.6
  33.3 0.9 copy-done.6
  34.2 3.9 %all-to-all-start.1 = ((bf16[32,2,3,16,128]{4,3,2,1,0:T(8,128)(2,1)}), bf16[32,2,3,16,128]{4,3,2,1,0:T(8,128)(2,1)S(1)}, u32[]{:S(2)}, u32[]{:S(2)}) async-start(bf16[32,2,3,16,128]{4,3,2,1,0:T(8,128)(2,1)} %bitcast.18), calls=%async_computation.1 | async-start | bytes 1572864 | tf_op jit(solution)/shard_map/all_to_all | solution.py:380
  38.1 0.0 copy-done.11
  38.1 0.1 broadcast_add_fusion
  38.2 0.1 iota_add_fusion
  38.3 0.1 add.38
  38.4 0.0 copy-done.10
  38.4 0.3 reduce-window.9
  38.7 0.1 slice.10
  38.8 0.1 slice_reduce_fusion
  38.9 0.1 add_bitcast_fusion
  39.0 0.2 select_reduce_fusion
  39.1 0.1 reshape.82
  39.2 0.1 broadcast_subtract_fusion
  39.3 0.1 tile.9.low_ref
  39.4 0.0 copy-done.4
  39.4 0.0 copy-done.5
  39.4 0.0 copy-done
  39.4 0.0 copy-start.2
  39.4 1.6 %copy-done.2 = bf16[128,8192]{1,0:T(8,128)(2,1)S(1)} copy-done((bf16[128,8192]{1,0:T(8,128)(2,1)S(1)}, bf16[128,8192]{1,0:T(8,128)(2,1)}, u32[]{:S(2)}) %copy-start.2) | copy-done | bytes 2097176
  41.0 1.6 %shard_map.96.stat_ref = f32[2,4,8,1024]{3,2,1,0:T(8,128)S(1)} custom-call(s32[2,1,256]{2,1,0:T(1,128)S(1)} %tile.9.low_ref, bf16[128,8192]{1,0:T(8,128)(2,1)S(1)} %copy-done, bf16[128,8192]{1,0:T(8,128)(2,1)S(1)} %copy-done.2, bf16[128,512]{1,0:T(8,128)(2,1)S(1)} %copy-done.4, bf16[128,512]{1,0:T(8,128)(2,1)S(1)} %copy-done.5, ...), custom_call_target="tpu_custom_call" | custom-call | tf_op jit(solution)/shard_map/pallas_call | solution.py:323
  42.6 17.6 %all-to-all-done.1 = bf16[32,2,3,16,128]{4,3,2,1,0:T(8,128)(2,1)S(1)} async-done(((bf16[32,2,3,16,128]{4,3,2,1,0:T(8,128)(2,1)}), bf16[32,2,3,16,128]{4,3,2,1,0:T(8,128)(2,1)S(1)}, u32[]{:S(2)}, u32[]{:S(2)}) %all-to-all-start.1) | async-done | bytes 786464 | tf_op jit(solution)/shard_map/all_to_all | solution.py:380
  60.3 0.0 copy-start.1
  60.3 6.9 %shard_map.97 = (bf16[2,4,4,2,3,16,128]{6,5,4,3,2,1,0:T(8,128)(2,1)S(1)}, s32[2,1,256]{2,1,0:T(1,128)S(1)}) custom-call(s32[2,1,256]{2,1,0:T(1,128)S(1)} %tile.9.low_ref, bf16[128,8192]{1,0:T(8,128)(2,1)} %q_ref.5, bf16[128,8192]{1,0:T(8,128)(2,1)} %g_ref.5, f32[2,4,8,1024]{3,2,1,0:T(8,128)S(1)} %shard_map.96.stat_ref, ...), custom_call_target="tpu_custom_call" | custom-call | tf_op jit(solution)/shard_map/pallas_call | solution.py:323
  67.1 0.0 copy-start.7
  67.2 0.9 copy-done.7
  68.1 4.9 %all-to-all-start.2 = ((bf16[32,2,3,16,128]{4,3,2,1,0:T(8,128)(2,1)}), bf16[32,2,3,16,128]{4,3,2,1,0:T(8,128)(2,1)}, u32[]{:S(2)}, u32[]{:S(2)}) async-start(bf16[32,2,3,16,128]{4,3,2,1,0:T(8,128)(2,1)} %bitcast.19), calls=%async_computation.2 | async-start | bytes 1572864 | tf_op jit(solution)/shard_map/all_to_all | solution.py:388
  73.0 0.0 copy-done.1
  73.0 0.0 copy-start.3
  73.0 1.6 %copy-done.3 = bf16[128,8192]{1,0:T(8,128)(2,1)S(1)} copy-done((bf16[128,8192]{1,0:T(8,128)(2,1)S(1)}, bf16[128,8192]{1,0:T(8,128)(2,1)}, u32[]{:S(2)}) %copy-start.3) | copy-done | bytes 2097176
  74.6 15.8 %shard_map.98 = (bf16[128,8192]{1,0:T(8,128)(2,1)}, bf16[128,8192]{1,0:T(8,128)(2,1)}, f32[128,512]{1,0:T(8,128)S(1)}, f32[128,512]{1,0:T(8,128)S(1)}) custom-call(s32[2,1,256]{2,1,0:T(1,128)S(1)} %get-tuple-element.22.low_ref, bf16[128,8192]{1,0:T(8,128)(2,1)S(1)} %copy-done.1, bf16[128,8192]{1,0:T(8,128)(2,1)S(1)} %copy-done.3, ...), custom_call_target="tpu_custom_call" | custom-call | tf_op jit(solution)/shard_map/pallas_call | solution.py:268
  90.4 0.0 copy-start.8
  90.4 0.7 copy-done.8
  91.1 4.4 %all-to-all-done.2 = bf16[32,2,3,16,128]{4,3,2,1,0:T(8,128)(2,1)} async-done(((bf16[32,2,3,16,128]{4,3,2,1,0:T(8,128)(2,1)}), bf16[32,2,3,16,128]{4,3,2,1,0:T(8,128)(2,1)}, u32[]{:S(2)}, u32[]{:S(2)}) %all-to-all-start.2) | async-done | bytes 786464 | tf_op jit(solution)/shard_map/all_to_all | solution.py:388
  95.5 0.0 copy-start.9
  95.5 1.3 %shard_map.100 = bf16[3,16,128]{2,1,0:T(8,128)(2,1)S(1)} custom-call(s32[64]{0:T(128)S(1)} %broadcast_clamp_fusion.place_ref, bf16[64,3,16,128]{3,2,1,0:T(8,128)(2,1)} %bitcast.8.parts_ref, f32[128,512]{1,0:T(8,128)S(1)} %get-tuple-element.28.after_ref.dk_ref), custom_call_target="tpu_custom_call" | custom-call | tf_op jit(solution)/shard_map/pallas_call | solution.py:323
  96.8 2.9 %collective-permute-start.1 = (bf16[3,16,128]{2,1,0:T(8,128)(2,1)S(1)}, bf16[3,16,128]{2,1,0:T(8,128)(2,1)S(1)}, u32[]{:S(2)}, u32[]{:S(2)}) collective-permute-start(bf16[3,16,128]{2,1,0:T(8,128)(2,1)S(1)} %shard_map.100), channel_id=1, source_target_pairs={{32,0},{64,32},{96,64},{128,96},{160,128},{192,160},{224,192},{33,... | collective-permute-start | bytes 36872 | tf_op jit(solution)/shard_map/ppermute | solution.py:400
  99.7 1.3 %shard_map.99 = (bf16[64,16,128]{2,1,0:T(8,128)(2,1)S(1)}, f32[3,16,128]{2,1,0:T(8,128)S(1)}) custom-call(s32[64]{0:T(128)S(1)} %broadcast_clamp_fusion.place_ref, bf16[64,3,16,128]{3,2,1,0:T(8,128)(2,1)} %bitcast.8.parts_ref), custom_call_target="tpu_custom_call" | custom-call | tf_op jit(solution)/shard_map/pallas_call | solution.py:323
  101.0 1.6 %collective-permute-done.1.next_ref = bf16[3,16,128]{2,1,0:T(8,128)(2,1)S(1)} collective-permute-done((bf16[3,16,128]{2,1,0:T(8,128)(2,1)S(1)}, bf16[3,16,128]{2,1,0:T(8,128)(2,1)S(1)}, u32[]{:S(2)}, u32[]{:S(2)}) %collective-permute-start.1) | collective-permute-done | bytes 12320 | tf_op jit(solution)/shard_map/ppermute | solution.py:400
  102.5 0.6 shard_map.101
  103.2 17.0 %all_to_all.20.pieces_ref = bf16[32,2,16,128]{3,2,1,0:T(8,128)(2,1)S(1)} all-to-all(bf16[32,2,16,128]{3,2,1,0:T(8,128)(2,1)S(1)} %bitcast.16), channel_id=1, replica_groups=mesh['grp'=8,'ctx'=32] {'ctx'}, dimensions={0} | all-to-all | bytes 524288 | tf_op jit(solution)/shard_map/all_to_all | solution.py:419
  120.2 0.0 copy-done.9
  120.2 0.7 shard_map.102
  (4 shorter events, 0.0 us)
Async XLA Ops:
  0.6 38.8 %copy-start.4 = (bf16[128,512]{1,0:T(8,128)(2,1)S(1)}, bf16[128,512]{1,0:T(8,128)(2,1)}, u32[]{:S(2)}) copy-start(bf16[128,512]{1,0:T(8,128)(2,1)} %k_ref.3) | copy-start | bytes 393220
  0.6 38.7 %copy-start.5 = (bf16[128,512]{1,0:T(8,128)(2,1)S(1)}, bf16[128,512]{1,0:T(8,128)(2,1)}, u32[]{:S(2)}) copy-start(bf16[128,512]{1,0:T(8,128)(2,1)} %v_ref.3) | copy-start | bytes 393220
  0.7 37.5 %copy-start.11 = (s32[64]{0:T(128)S(1)}, s32[64]{0:T(128)}, u32[]{:S(2)}) copy-start(s32[64]{0:T(128)} %param.11) | copy-start | bytes 772
  0.7 37.7 %copy-start.10 = (s32[682]{0:T(1024)S(1)}, s32[682]{0:T(1024)}, u32[]{:S(2)}) copy-start(s32[682]{0:T(1024)} %param.10) | copy-start | bytes 8188
  0.7 38.7 %copy-start = (bf16[128,8192]{1,0:T(8,128)(2,1)S(1)}, bf16[128,8192]{1,0:T(8,128)(2,1)}, u32[]{:S(2)}) copy-start(bf16[128,8192]{1,0:T(8,128)(2,1)} %q_ref.5) | copy-start | bytes 6291460
  2.6 23.2 %all-to-all-start = ((bf16[32,2,16,128]{3,2,1,0:T(8,128)(2,1)}), bf16[32,2,16,128]{3,2,1,0:T(8,128)(2,1)S(1)}, u32[]{:S(2)}, u32[]{:S(2)}) async-start(bf16[32,2,16,128]{3,2,1,0:T(8,128)(2,1)} %shard_map.93), calls=%async_computation | async-start | bytes 524288 | tf_op jit(solution)/shard_map/all_to_all | solution.py:362
  26.4 6.3 %collective-permute-start = (bf16[3,16,128]{2,1,0:T(8,128)(2,1)S(1)}, bf16[3,16,128]{2,1,0:T(8,128)(2,1)S(1)}, u32[]{:S(2)}, u32[]{:S(2)}) collective-permute-start(bf16[3,16,128]{2,1,0:T(8,128)(2,1)S(1)} %get-tuple-element.19), channel_id=1, source_target_pairs={{0,32},{32,64},{64,96},{96,128},{128,160},{160,192},{192,224},{1,3... | collective-permute-start | bytes 36872 | tf_op jit(solution)/shard_map/ppermute | solution.py:370
  33.3 0.9 copy-start.6
  34.2 26.1 %all-to-all-start.1 = ((bf16[32,2,3,16,128]{4,3,2,1,0:T(8,128)(2,1)}), bf16[32,2,3,16,128]{4,3,2,1,0:T(8,128)(2,1)S(1)}, u32[]{:S(2)}, u32[]{:S(2)}) async-start(bf16[32,2,3,16,128]{4,3,2,1,0:T(8,128)(2,1)} %bitcast.18), calls=%async_computation.1 | async-start | bytes 1572864 | tf_op jit(solution)/shard_map/all_to_all | solution.py:380
  39.4 1.6 %copy-start.2 = (bf16[128,8192]{1,0:T(8,128)(2,1)S(1)}, bf16[128,8192]{1,0:T(8,128)(2,1)}, u32[]{:S(2)}) copy-start(bf16[128,8192]{1,0:T(8,128)(2,1)} %g_ref.5) | copy-start | bytes 6291460
  60.3 12.7 %copy-start.1 = (bf16[128,8192]{1,0:T(8,128)(2,1)S(1)}, bf16[128,8192]{1,0:T(8,128)(2,1)}, u32[]{:S(2)}) copy-start(bf16[128,8192]{1,0:T(8,128)(2,1)} %q_ref.5) | copy-start | bytes 6291460
  67.1 0.9 copy-start.7
  68.1 27.4 %all-to-all-start.2 = ((bf16[32,2,3,16,128]{4,3,2,1,0:T(8,128)(2,1)}), bf16[32,2,3,16,128]{4,3,2,1,0:T(8,128)(2,1)}, u32[]{:S(2)}, u32[]{:S(2)}) async-start(bf16[32,2,3,16,128]{4,3,2,1,0:T(8,128)(2,1)} %bitcast.19), calls=%async_computation.2 | async-start | bytes 1572864 | tf_op jit(solution)/shard_map/all_to_all | solution.py:388
  73.0 1.6 %copy-start.3 = (bf16[128,8192]{1,0:T(8,128)(2,1)S(1)}, bf16[128,8192]{1,0:T(8,128)(2,1)}, u32[]{:S(2)}) copy-start(bf16[128,8192]{1,0:T(8,128)(2,1)} %g_ref.5) | copy-start | bytes 6291460
  90.4 0.7 copy-start.8
  95.5 24.7 %copy-start.9 = (f32[128,512]{1,0:T(8,128)S(1)}, f32[128,512]{1,0:T(8,128)}, u32[]{:S(2)}) copy-start(f32[128,512]{1,0:T(8,128)} %copy-done.8) | copy-start | bytes 786436
  96.8 5.8 %collective-permute-start.1 = (bf16[3,16,128]{2,1,0:T(8,128)(2,1)S(1)}, bf16[3,16,128]{2,1,0:T(8,128)(2,1)S(1)}, u32[]{:S(2)}, u32[]{:S(2)}) collective-permute-start(bf16[3,16,128]{2,1,0:T(8,128)(2,1)S(1)} %shard_map.100), channel_id=1, source_target_pairs={{32,0},{64,32},{96,64},{128,96},{160,128},{192,160},{224,192},{33,... | collective-permute-start | bytes 36872 | tf_op jit(solution)/shard_map/ppermute | solution.py:400

commit v3 on v2

--- a/solution.py
+++ b/solution.py
@@ -68,10 +68,21 @@
     )
 
 
-def head_kernel(place_ref, parts_ref, after_ref, out_ref, slot_of):
+def head_kernel(place_ref, parts_ref, after_ref, out_ref, slot_of, early, sems):
     slots_of(place_ref, slot_of)
+    copies = [
+        pltpu.make_async_copy(parts_ref.at[slot_of[i]], early.at[i], sems.at[i])
+        for i in range(BEFORE)
+    ]
+    for copy in copies:
+        copy.start()
+    for copy in copies:
+        copy.wait()
     for back in range(BEFORE):
-        out_ref[back] = part_sum(slot_of, parts_ref, back - BEFORE).astype(jnp.bfloat16)
+        total = sum(
+            early[block, back - block].astype(jnp.float32) for block in range(back + 1)
+        )
+        out_ref[back] = total.astype(jnp.bfloat16)
 
 
 def sum_kernel(place_ref, parts_ref, sums_ref, tail_ref, slot_of):
@@ -116,14 +127,6 @@
 NT = (((1,), (1,)), ((), ()))
 NN = (((1,), (0,)), ((), ()))
 dot = functools.partial(lax.dot_general, preferred_element_type=jnp.float32)
-
-
-def mask_to(bias_ref, low_ref, first_key):
-    keys, lanes = bias_ref.shape
-    key_index = first_key + lax.broadcasted_iota(jnp.int32, (keys, lanes), 0)
-    query_index = lax.broadcasted_iota(jnp.int32, (keys, lanes), 1) % BLOCK
-    allowed = (key_index <= query_index + LIMIT) & (key_index >= low_ref[0])
-    bias_ref[...] = jnp.where(allowed, 0.0, -1e30)
 
 
 def far_rows(far_ref, tensor, head, half):
@@ -219,64 +222,67 @@
 
 
 def rest_kernel(
-    low_ref, q_ref, g_ref, k_ref, v_ref, far_ref, att_ref, dq_ref, dk_ref, dv_ref, bias_ref
+    low_ref, q_ref, g_ref, k_ref, v_ref, far_ref, att_out_ref, dq_out_ref, dk_ref, dv_ref,
+    bias_ref, q_rows, g_rows, att_rows, dq_rows, load_sems, store_sems,
 ):
-    half = pl.program_id(0)
-    head = pl.program_id(1)
-
-    @pl.when(head == 0)
-    def _():
-        mask_to(bias_ref, low_ref, 0)
-
-    keys = jnp.concatenate(far_rows(far_ref, 0, head, half) + [k_ref[...]], axis=0)
-    values = jnp.concatenate(far_rows(far_ref, 1, head, half) + [v_ref[...]], axis=0)
-    keys_t = keys.T
-    values_t = values.T
-
-    def put(ref, first, cols):
+    loads = [
+        [
+            pltpu.make_async_copy(
+                ref.at[pl.ds(half * BLOCK, BLOCK)],
+                rows.at[pl.ds(half * BLOCK, BLOCK)],
+                load_sems.at[half, i],
+            )
+            for i, (ref, rows) in enumerate(((q_ref, q_rows), (g_ref, g_rows)))
+        ]
+        for half in range(2)
+    ]
+    for load in loads[0] + loads[1]:
+        load.start()
+    key_index = lax.broadcasted_iota(jnp.int32, (LIMIT + BLOCK, CHUNK * BLOCK), 0)
+    query_index = lax.broadcasted_iota(jnp.int32, key_index.shape, 1) % BLOCK
+    for half in range(2):
+        allowed = (key_index <= query_index + LIMIT) & (key_index >= low_ref[half])
+        bias = jnp.where(allowed, 0.0, -1e30)
+        bias_ref[half] = jnp.concatenate([bias] * (GROUP_WIDTH // CHUNK), axis=1)
+
+    def put(ref, cols):
         rows = cols.T.astype(jnp.bfloat16)
-        for i in range(CHUNK):
-            ref[:, pl.ds((first + i) * HEAD, HEAD)] = rows[i * BLOCK : (i + 1) * BLOCK]
-
-    key_grad = jnp.zeros((BLOCK, HEAD), jnp.float32)
-    value_grad = jnp.zeros((BLOCK, HEAD), jnp.float32)
-    for first in range(0, GROUP_WIDTH, CHUNK):
-        query = rows_of(q_ref, first)
-        grad = rows_of(g_ref, first)
-        scores = dot(keys, query, NT) * (SCALE * LOG2E) + bias_ref[...]
-        dprob = dot(values, grad, NT)
-        raw = jnp.exp2(scores - jnp.max(scores, axis=0, keepdims=True))
-        weights = raw * (1.0 / jnp.sum(raw, axis=0, keepdims=True))
-        weights_low = weights.astype(jnp.bfloat16)
-        put(att_ref, first, dot(values_t, weights_low, NN))
-        delta = jnp.sum(weights * dprob, axis=0, keepdims=True)
-        dscore = (weights * (dprob - delta)).astype(jnp.bfloat16)
-        put(dq_ref, first, dot(keys_t, dscore, NN) * SCALE)
-        key_grad += dot(dscore[LIMIT:], query, NN)
-        value_grad += dot(weights_low[LIMIT:], grad, NN)
-    dk_ref[...] = key_grad * SCALE
-    dv_ref[...] = value_grad
-
-
-LOW = pl.BlockSpec((1, 1, CHUNK * BLOCK), lambda j, h: (j, 0, 0))
-WIDE = pl.BlockSpec((BLOCK, GROUP_WIDTH * HEAD), lambda j, h: (j, h))
-NARROW = pl.BlockSpec((BLOCK, HEAD), lambda j, h: (j, h))
-STAT = pl.BlockSpec((1, 1, 8, GROUP_WIDTH * BLOCK), lambda j, h: (j, h, 0, 0))
-
-
-def grid_call(kernel, keys, in_specs, out_specs, out_shape, *args):
-    return pl.pallas_call(
-        kernel,
-        grid=(2, KV_HEADS),
-        in_specs=in_specs,
-        out_specs=out_specs,
-        out_shape=out_shape,
-        scratch_shapes=[pltpu.VMEM((keys, CHUNK * BLOCK), jnp.float32)],
-        compiler_params=pltpu.CompilerParams(
-            dimension_semantics=("arbitrary", "arbitrary"),
-            vmem_limit_bytes=24 * MIB,
-        ),
-    )(*args)
+        for i in range(GROUP_WIDTH):
+            ref[:, pl.ds(i * HEAD, HEAD)] = rows[i * BLOCK : (i + 1) * BLOCK]
+
+    stores = []
+    for half in range(2):
+        rows = pl.ds(half * BLOCK, BLOCK)
+        for load in loads[half]:
+            load.wait()
+        for head in range(KV_HEADS):
+            cols = pl.ds(head * HEAD, HEAD)
+            wide = pl.ds(head * GROUP_WIDTH * HEAD, GROUP_WIDTH * HEAD)
+            keys = jnp.concatenate(far_rows(far_ref, 0, head, half) + [k_ref[rows, cols]], axis=0)
+            values = jnp.concatenate(
+                far_rows(far_ref, 1, head, half) + [v_ref[rows, cols]], axis=0
+            )
+            query = rows_of(q_rows.at[rows], head * GROUP_WIDTH, GROUP_WIDTH)
+            grad = rows_of(g_rows.at[rows], head * GROUP_WIDTH, GROUP_WIDTH)
+            scores = dot(keys, query, NT) * (SCALE * LOG2E) + bias_ref[half]
+            dprob = dot(values, grad, NT)
+            raw = jnp.exp2(scores - jnp.max(scores, axis=0, keepdims=True))
+            weights = raw * (1.0 / jnp.sum(raw, axis=0, keepdims=True))
+            weights_low = weights.astype(jnp.bfloat16)
+            put(att_rows.at[rows, wide], dot(values.T, weights_low, NN))
+            delta = jnp.sum(weights * dprob, axis=0, keepdims=True)
+            dscore = (weights * (dprob - delta)).astype(jnp.bfloat16)
+            put(dq_rows.at[rows, wide], dot(keys.T, dscore, NN) * SCALE)
+            dk_ref[rows, cols] = dot(dscore[LIMIT:], query, NN) * SCALE
+            dv_ref[rows, cols] = dot(weights_low[LIMIT:], grad, NN)
+            for i, (held, out) in enumerate(((att_rows, att_out_ref), (dq_rows, dq_out_ref))):
+                store = pltpu.make_async_copy(
+                    held.at[rows, wide], out.at[rows, wide], store_sems.at[half, head, i]
+                )
+                store.start()
+                stores.append(store)
+    for store in stores:
+        store.wait()
 
 
 def attend_own(low, queries, out_grad, key_tensor, value_tensor, after):
@@ -312,10 +318,19 @@
 def attend_rest(low, queries, out_grad, key_tensor, value_tensor, far):
     wide = jax.ShapeDtypeStruct(queries.shape, jnp.bfloat16)
     narrow = jax.ShapeDtypeStruct(key_tensor.shape, jnp.float32)
-    return grid_call(
-        rest_kernel, LIMIT + BLOCK, [LOW, WIDE, WIDE, NARROW, NARROW, VMEM],
-        [WIDE, WIDE, NARROW, NARROW], [wide, wide, narrow, narrow],
+    return call(
+        rest_kernel,
+        [wide, wide, narrow, narrow],
+        [VMEM, ANY, ANY, VMEM, VMEM, VMEM],
         low, queries, out_grad, key_tensor, value_tensor, far,
+        out_specs=[ANY, ANY, VMEM, VMEM],
+        scratch=[
+            pltpu.VMEM((2, LIMIT + BLOCK, GROUP_WIDTH * BLOCK), jnp.float32),
+            *[pltpu.VMEM(queries.shape, jnp.bfloat16)] * 4,
+            pltpu.SemaphoreType.DMA((2, 2)),
+            pltpu.SemaphoreType.DMA((2, KV_HEADS, 2)),
+        ],
+        limit=52 * MIB,
     )
 
 
@@ -391,11 +406,15 @@
     (ahead,) = call(
         head_kernel,
         [bf16((BEFORE, *tile))],
-        [SMEM, VMEM, ANY],
+        [SMEM, ANY, ANY],
         place,
         parts,
         own_k,
-        scratch=[slot_of],
+        scratch=[
+            slot_of,
+            pltpu.VMEM((BEFORE, BEFORE, *tile), jnp.bfloat16),
+            pltpu.SemaphoreType.DMA((BEFORE,)),
+        ],
     )
     behind = lax.ppermute(ahead, "grp", [(i + 1, i) for i in range(grp_count - 1)])
     sums, tail = call(

time: 122 us -> 121 us (level)
  waiting for transfers between devices: 34.9 us -> 42.8 us
  Pallas kernels: 30.2 us -> 24.5 us
  local copies, waits for them, and re-layouts: 6.16 us -> 2.94 us
    pallas_call x1 -> x0, Pallas kernels: 15.8 us -> none  [grid_call(): pl.pallas_call(kernel, grid=(2, KV_HEADS), in_specs=in_specs, out_specs=o...]
    pallas_call x9 -> x10, Pallas kernels: 14.4 us -> 24.5 us  [call(): pl.pallas_call(kernel, in_specs=specs, out_specs=out_specs or [VMEM] * le...]
    all_to_all x1, waiting for transfers between devices: 4.43 us -> 11.6 us  [body(): parts = exchange(far_grad.reshape(ctx_count, 2, BEFORE, *tile))]
    unnamed x24 -> x14, local copies, waits for them, and re-layouts: 5.71 us -> 2.49 us
  transfers between devices with their start and end apart: 5 -> 5, of which waited for: 5 -> 5; matrix products, arithmetic and copies ran while one was open for 2% -> 2% of each run, Pallas kernels for 15% -> 11%
where the time goes in v3:
time: 121 us; the launch traced here: 120 us
  waiting for transfers between devices  42.8 us (35%)
  starting transfers between devices  29.5 us (24%)
  Pallas kernels  24.5 us (20%)
  blocking collectives  17.2 us (14%)
  local copies, waits for them, and re-layouts  2.94 us (2%)
  other arithmetic  2.6 us (2%)
    pallas_call x10, Pallas kernels, call(): pl.pallas_call(kernel, in_specs=specs, out_specs=out_specs or [VMEM] * le...  24.5 us
    all_to_all x1, waiting for transfers between devices, body(): far = exchange(wanted.reshape(ctx_count, 2, BEFORE, *tile))  17.6 us
    all_to_all x1, blocking collectives, body(): sums = exchange(sums.reshape(ctx_count, 2, *tile))  17.2 us
    all_to_all x1, starting transfers between devices, body(): pieces = exchange(packed).reshape(SLOTS, *tile)  12 us
    all_to_all x1, waiting for transfers between devices, body(): parts = exchange(far_grad.reshape(ctx_count, 2, BEFORE, *tile))  11.6 us
    all_to_all x1, waiting for transfers between devices, body(): pieces = exchange(packed).reshape(SLOTS, *tile)  10.5 us
    ppermute x1, starting transfers between devices, body(): prev = lax.ppermute(last, 'grp', [(i, i + 1) for i in range(grp_count - 1)])  5.46 us
    all_to_all x1, starting transfers between devices, body(): parts = exchange(far_grad.reshape(ctx_count, 2, BEFORE, *tile))  4.98 us
  transfers between devices with their start and end apart: 5, of which 5 were waited for; matrix products, arithmetic and copies ran while one was open for 2% of the time, Pallas kernels for 11%

profile of v3, /device:TPU:1, one launch (start us, length us, event | category | flops | bytes accessed | tf_op | source)
XLA Modules:
  0.0 120.2 jit_solution(1318116202611123236)
XLA Ops:
  0.6 0.0 copy-start.2
  0.6 0.0 copy-start.3
  0.7 0.0 copy-start.6
  0.7 0.0 copy-start.5
  0.7 0.0 copy-start
  0.7 1.1 pad_maximum_fusion.rows_ref
  1.8 0.7 shard_map.93
  2.6 12.0 %all-to-all-start = ((bf16[32,2,16,128]{3,2,1,0:T(8,128)(2,1)}), bf16[32,2,16,128]{3,2,1,0:T(8,128)(2,1)S(1)}, u32[]{:S(2)}, u32[]{:S(2)}) async-start(bf16[32,2,16,128]{3,2,1,0:T(8,128)(2,1)} %shard_map.93), calls=%async_computation | async-start | bytes 524288 | tf_op jit(solution)/shard_map/all_to_all | solution.py:377
  14.6 0.7 broadcast_clamp_fusion.place_ref
  15.3 10.5 %all-to-all-done = bf16[32,2,16,128]{3,2,1,0:T(8,128)(2,1)S(1)} async-done(((bf16[32,2,16,128]{3,2,1,0:T(8,128)(2,1)}), bf16[32,2,16,128]{3,2,1,0:T(8,128)(2,1)S(1)}, u32[]{:S(2)}, u32[]{:S(2)}) %all-to-all-start) | async-done | bytes 262176 | tf_op jit(solution)/shard_map/all_to_all | solution.py:377
  25.8 0.6 shard_map.94
  26.4 5.5 %collective-permute-start = (bf16[3,16,128]{2,1,0:T(8,128)(2,1)S(1)}, bf16[3,16,128]{2,1,0:T(8,128)(2,1)S(1)}, u32[]{:S(2)}, u32[]{:S(2)}) collective-permute-start(bf16[3,16,128]{2,1,0:T(8,128)(2,1)S(1)} %get-tuple-element.19), channel_id=1, source_target_pairs={{0,32},{32,64},{64,96},{96,128},{128,160},{160,192},{192,224},{1,3... | collective-permute-start | bytes 36872 | tf_op jit(solution)/shard_map/ppermute | solution.py:385
  31.9 0.8 collective-permute-done.prev_ref
  32.7 0.6 shard_map.95
  33.3 0.0 copy-start.4
  33.3 0.9 copy-done.4
  34.2 3.9 %all-to-all-start.1 = ((bf16[32,2,3,16,128]{4,3,2,1,0:T(8,128)(2,1)}), bf16[32,2,3,16,128]{4,3,2,1,0:T(8,128)(2,1)S(1)}, u32[]{:S(2)}, u32[]{:S(2)}) async-start(bf16[32,2,3,16,128]{4,3,2,1,0:T(8,128)(2,1)} %bitcast.20), calls=%async_computation.1 | async-start | bytes 1572864 | tf_op jit(solution)/shard_map/all_to_all | solution.py:395
  38.1 0.0 copy-done.6
  38.1 0.1 broadcast_add_fusion
  38.2 0.1 iota_add_fusion
  38.3 0.1 add.38
  38.4 0.0 copy-done.5
  38.4 0.3 reduce-window.9
  38.7 0.1 slice.10
  38.8 0.1 slice_reduce_fusion
  38.9 0.1 add_bitcast_fusion
  39.0 0.2 select_reduce_fusion
  39.1 0.1 reshape.82
  39.2 0.1 broadcast_subtract_fusion
  39.3 0.1 tile.9.low_ref
  39.4 0.0 copy-done.2
  39.4 0.0 copy-done.3
  39.4 0.0 copy-done
  39.4 0.0 copy-start.1
  39.4 1.6 %copy-done.1 = bf16[128,8192]{1,0:T(8,128)(2,1)S(1)} copy-done((bf16[128,8192]{1,0:T(8,128)(2,1)S(1)}, bf16[128,8192]{1,0:T(8,128)(2,1)}, u32[]{:S(2)}) %copy-start.1) | copy-done | bytes 2097176
  41.0 1.6 %shard_map.96.stat_ref = f32[2,4,8,1024]{3,2,1,0:T(8,128)S(1)} custom-call(s32[2,1,256]{2,1,0:T(1,128)S(1)} %tile.9.low_ref, bf16[128,8192]{1,0:T(8,128)(2,1)S(1)} %copy-done, bf16[128,8192]{1,0:T(8,128)(2,1)S(1)} %copy-done.1, bf16[128,512]{1,0:T(8,128)(2,1)S(1)} %copy-done.2, bf16[128,512]{1,0:T(8,128)(2,1)S(1)} %copy-done.3, ...), custom_call_target="tpu_custom_call" | custom-call | tf_op jit(solution)/shard_map/pallas_call | solution.py:338
  42.6 17.6 %all-to-all-done.1 = bf16[32,2,3,16,128]{4,3,2,1,0:T(8,128)(2,1)S(1)} async-done(((bf16[32,2,3,16,128]{4,3,2,1,0:T(8,128)(2,1)}), bf16[32,2,3,16,128]{4,3,2,1,0:T(8,128)(2,1)S(1)}, u32[]{:S(2)}, u32[]{:S(2)}) %all-to-all-start.1) | async-done | bytes 786464 | tf_op jit(solution)/shard_map/all_to_all | solution.py:395
  60.3 7.6 %shard_map.97 = (bf16[2,4,4,2,3,16,128]{6,5,4,3,2,1,0:T(8,128)(2,1)}, s32[2,1,256]{2,1,0:T(1,128)S(1)}) custom-call(s32[2,1,256]{2,1,0:T(1,128)S(1)} %tile.9.low_ref, bf16[128,8192]{1,0:T(8,128)(2,1)} %q_ref.5, bf16[128,8192]{1,0:T(8,128)(2,1)} %g_ref.5, f32[2,4,8,1024]{3,2,1,0:T(8,128)S(1)} %shard_map.96.stat_ref, ...), custom_call_target="tpu_custom_call" | custom-call | tf_op jit(solution)/shard_map/pallas_call | solution.py:338
  67.9 5.0 %all-to-all-start.2 = ((bf16[32,2,3,16,128]{4,3,2,1,0:T(8,128)(2,1)}), bf16[32,2,3,16,128]{4,3,2,1,0:T(8,128)(2,1)S(1)}, u32[]{:S(2)}, u32[]{:S(2)}) async-start(bf16[32,2,3,16,128]{4,3,2,1,0:T(8,128)(2,1)} %bitcast.7), calls=%async_computation.2 | async-start | bytes 1572864 | tf_op jit(solution)/shard_map/all_to_all | solution.py:403
  72.9 10.5 %shard_map.98 = (bf16[128,8192]{1,0:T(8,128)(2,1)}, bf16[128,8192]{1,0:T(8,128)(2,1)}, f32[128,512]{1,0:T(8,128)S(1)}, f32[128,512]{1,0:T(8,128)S(1)}) custom-call(s32[2,1,256]{2,1,0:T(1,128)S(1)} %get-tuple-element.22.low_ref, bf16[128,8192]{1,0:T(8,128)(2,1)} %q_ref.5, bf16[128,8192]{1,0:T(8,128)(2,1)} %g_ref.5, bf16[128,512]{1,0:T(8,128)(2,1)S(1)} %copy-done.2, ...), custom_call_target="tpu_custom_call" | custom-call | tf_op jit(solution)/shard_map/pallas_call | solution.py:338
  83.4 11.6 %all-to-all-done.2 = bf16[32,2,3,16,128]{4,3,2,1,0:T(8,128)(2,1)S(1)} async-done(((bf16[32,2,3,16,128]{4,3,2,1,0:T(8,128)(2,1)}), bf16[32,2,3,16,128]{4,3,2,1,0:T(8,128)(2,1)S(1)}, u32[]{:S(2)}, u32[]{:S(2)}) %all-to-all-start.2) | async-done | bytes 786464 | tf_op jit(solution)/shard_map/all_to_all | solution.py:403
  95.0 0.7 shard_map.100
  95.7 3.1 %collective-permute-start.1 = (bf16[3,16,128]{2,1,0:T(8,128)(2,1)S(1)}, bf16[3,16,128]{2,1,0:T(8,128)(2,1)S(1)}, u32[]{:S(2)}, u32[]{:S(2)}) collective-permute-start(bf16[3,16,128]{2,1,0:T(8,128)(2,1)S(1)} %shard_map.100), channel_id=1, source_target_pairs={{32,0},{64,32},{96,64},{128,96},{160,128},{192,160},{224,192},{33,... | collective-permute-start | bytes 36872 | tf_op jit(solution)/shard_map/ppermute | solution.py:419
  98.8 0.7 shard_map.99
  99.5 2.2 %collective-permute-done.1.next_ref = bf16[3,16,128]{2,1,0:T(8,128)(2,1)S(1)} collective-permute-done((bf16[3,16,128]{2,1,0:T(8,128)(2,1)S(1)}, bf16[3,16,128]{2,1,0:T(8,128)(2,1)S(1)}, u32[]{:S(2)}, u32[]{:S(2)}) %collective-permute-start.1) | collective-permute-done | bytes 12320 | tf_op jit(solution)/shard_map/ppermute | solution.py:419
  101.7 0.6 shard_map.101
  102.3 17.2 %all_to_all.20.pieces_ref = bf16[32,2,16,128]{3,2,1,0:T(8,128)(2,1)S(1)} all-to-all(bf16[32,2,16,128]{3,2,1,0:T(8,128)(2,1)S(1)} %bitcast.18), channel_id=1, replica_groups=mesh['grp'=8,'ctx'=32] {'ctx'}, dimensions={0} | all-to-all | bytes 524288 | tf_op jit(solution)/shard_map/all_to_all | solution.py:438
  119.5 0.7 shard_map.102
  (4 shorter events, 0.0 us)
Async XLA Ops:
  0.6 38.8 %copy-start.2 = (bf16[128,512]{1,0:T(8,128)(2,1)S(1)}, bf16[128,512]{1,0:T(8,128)(2,1)}, u32[]{:S(2)}) copy-start(bf16[128,512]{1,0:T(8,128)(2,1)} %k_ref.3) | copy-start | bytes 393220
  0.6 38.7 %copy-start.3 = (bf16[128,512]{1,0:T(8,128)(2,1)S(1)}, bf16[128,512]{1,0:T(8,128)(2,1)}, u32[]{:S(2)}) copy-start(bf16[128,512]{1,0:T(8,128)(2,1)} %v_ref.3) | copy-start | bytes 393220
  0.7 37.5 %copy-start.6 = (s32[64]{0:T(128)S(1)}, s32[64]{0:T(128)}, u32[]{:S(2)}) copy-start(s32[64]{0:T(128)} %param.11) | copy-start | bytes 772
  0.7 37.7 %copy-start.5 = (s32[682]{0:T(1024)S(1)}, s32[682]{0:T(1024)}, u32[]{:S(2)}) copy-start(s32[682]{0:T(1024)} %param.10) | copy-start | bytes 8188
  0.7 38.7 %copy-start = (bf16[128,8192]{1,0:T(8,128)(2,1)S(1)}, bf16[128,8192]{1,0:T(8,128)(2,1)}, u32[]{:S(2)}) copy-start(bf16[128,8192]{1,0:T(8,128)(2,1)} %q_ref.5) | copy-start | bytes 6291460
  2.6 23.2 %all-to-all-start = ((bf16[32,2,16,128]{3,2,1,0:T(8,128)(2,1)}), bf16[32,2,16,128]{3,2,1,0:T(8,128)(2,1)S(1)}, u32[]{:S(2)}, u32[]{:S(2)}) async-start(bf16[32,2,16,128]{3,2,1,0:T(8,128)(2,1)} %shard_map.93), calls=%async_computation | async-start | bytes 524288 | tf_op jit(solution)/shard_map/all_to_all | solution.py:377
  26.4 6.3 %collective-permute-start = (bf16[3,16,128]{2,1,0:T(8,128)(2,1)S(1)}, bf16[3,16,128]{2,1,0:T(8,128)(2,1)S(1)}, u32[]{:S(2)}, u32[]{:S(2)}) collective-permute-start(bf16[3,16,128]{2,1,0:T(8,128)(2,1)S(1)} %get-tuple-element.19), channel_id=1, source_target_pairs={{0,32},{32,64},{64,96},{96,128},{128,160},{160,192},{192,224},{1,3... | collective-permute-start | bytes 36872 | tf_op jit(solution)/shard_map/ppermute | solution.py:385
  33.3 0.9 copy-start.4
  34.2 26.1 %all-to-all-start.1 = ((bf16[32,2,3,16,128]{4,3,2,1,0:T(8,128)(2,1)}), bf16[32,2,3,16,128]{4,3,2,1,0:T(8,128)(2,1)S(1)}, u32[]{:S(2)}, u32[]{:S(2)}) async-start(bf16[32,2,3,16,128]{4,3,2,1,0:T(8,128)(2,1)} %bitcast.20), calls=%async_computation.1 | async-start | bytes 1572864 | tf_op jit(solution)/shard_map/all_to_all | solution.py:395
  39.4 1.6 %copy-start.1 = (bf16[128,8192]{1,0:T(8,128)(2,1)S(1)}, bf16[128,8192]{1,0:T(8,128)(2,1)}, u32[]{:S(2)}) copy-start(bf16[128,8192]{1,0:T(8,128)(2,1)} %g_ref.5) | copy-start | bytes 6291460
  67.9 27.1 %all-to-all-start.2 = ((bf16[32,2,3,16,128]{4,3,2,1,0:T(8,128)(2,1)}), bf16[32,2,3,16,128]{4,3,2,1,0:T(8,128)(2,1)S(1)}, u32[]{:S(2)}, u32[]{:S(2)}) async-start(bf16[32,2,3,16,128]{4,3,2,1,0:T(8,128)(2,1)} %bitcast.7), calls=%async_computation.2 | async-start | bytes 1572864 | tf_op jit(solution)/shard_map/all_to_all | solution.py:403
  95.7 6.0 %collective-permute-start.1 = (bf16[3,16,128]{2,1,0:T(8,128)(2,1)S(1)}, bf16[3,16,128]{2,1,0:T(8,128)(2,1)S(1)}, u32[]{:S(2)}, u32[]{:S(2)}) collective-permute-start(bf16[3,16,128]{2,1,0:T(8,128)(2,1)S(1)} %shard_map.100), channel_id=1, source_target_pairs={{32,0},{64,32},{96,64},{128,96},{160,128},{192,160},{224,192},{33,... | collective-permute-start | bytes 36872 | tf_op jit(solution)/shard_map/ppermute | solution.py:419

commit v4 on v3

--- a/solution.py
+++ b/solution.py
@@ -47,12 +47,18 @@
     last_ref[...] = ordered_ref[SLOTS - BEFORE :]
 
 
-def spread_kernel(place_ref, ordered_ref, prev_ref, out_ref, done_ref, whole):
+def spread_kernel(
+    late_ref, place_ref, ordered_ref, prev_ref, low_ref, q_ref, g_ref, kv_ref,
+    out_ref, stat_ref, whole, *scratch,
+):
     whole[:BEFORE] = prev_ref[...]
     whole[BEFORE:] = ordered_ref[...]
-    done_ref[...] = jnp.zeros_like(done_ref)
     for slot in range(SLOTS):
         out_ref[slot] = whole[pl.ds(place_ref[slot], BEFORE)]
+
+    @pl.when(late_ref[0] != 0)
+    def _():
+        own_stats(low_ref, q_ref, g_ref, kv_ref, stat_ref, *scratch)
 
 
 def slots_of(place_ref, slot_of):
@@ -137,9 +143,18 @@
     ]
 
 
-def own_kernel(
-    low_ref, q_ref, g_ref, k_ref, v_ref, after_ref, stat_ref, bias_ref
-):
+def own_stats(low_ref, q_ref, g_ref, kv_ref, stat_ref, bias_ref, rows_ref, sems):
+    loads = [
+        [
+            pltpu.make_async_copy(
+                ref.at[pl.ds(half * BLOCK, BLOCK)], rows_ref.at[half, i], sems.at[half, i]
+            )
+            for i, ref in enumerate((q_ref, g_ref))
+        ]
+        for half in range(2)
+    ]
+    for load in loads[0] + loads[1]:
+        load.start()
     key_index = LIMIT + lax.broadcasted_iota(jnp.int32, bias_ref.shape[1:], 0)
     query_index = lax.broadcasted_iota(jnp.int32, bias_ref.shape[1:], 1) % BLOCK
     for half in range(2):
@@ -148,19 +163,43 @@
 
     for half in range(2):
         rows = pl.ds(half * BLOCK, BLOCK)
+        for load in loads[half]:
+            load.wait()
         for head in range(KV_HEADS):
             cols = pl.ds(head * HEAD, HEAD)
             for first in range(0, GROUP_WIDTH, CHUNK):
                 lanes = pl.ds(first * BLOCK, CHUNK * BLOCK)
-                query = rows_of(q_ref.at[rows], head * GROUP_WIDTH + first)
-                grad = rows_of(g_ref.at[rows], head * GROUP_WIDTH + first)
-                scores = dot(k_ref[rows, cols], query, NT) * (SCALE * LOG2E) + bias_ref[half]
-                dprob = dot(v_ref[rows, cols], grad, NT)
+                query = rows_of(rows_ref.at[half, 0], head * GROUP_WIDTH + first)
+                grad = rows_of(rows_ref.at[half, 1], head * GROUP_WIDTH + first)
+                scores = dot(kv_ref[0, rows, cols], query, NT) * (SCALE * LOG2E) + bias_ref[half]
+                dprob = dot(kv_ref[1, rows, cols], grad, NT)
                 top = jnp.max(scores, axis=0, keepdims=True)
                 raw = jnp.exp2(scores - top)
                 stat_ref[half, head, 0:1, lanes] = top
                 stat_ref[half, head, 1:2, lanes] = jnp.sum(raw, axis=0, keepdims=True)
                 stat_ref[half, head, 2:3, lanes] = jnp.sum(raw * dprob, axis=0, keepdims=True)
+
+
+OWN_SCRATCH = [
+    pltpu.VMEM((2, BLOCK, CHUNK * BLOCK), jnp.float32),
+    pltpu.VMEM((2, 2, BLOCK, KV_HEADS * GROUP_WIDTH * HEAD), jnp.bfloat16),
+    pltpu.SemaphoreType.DMA((2, 2)),
+]
+STAT = jax.ShapeDtypeStruct((2, KV_HEADS, 8, GROUP_WIDTH * BLOCK), jnp.float32)
+
+
+def own_kernel(
+    late_ref, before_ref, low_ref, q_ref, g_ref, kv_ref, stat_ref, *scratch
+):
+    late = late_ref[0]
+
+    @pl.when(late == 0)
+    def _():
+        own_stats(low_ref, q_ref, g_ref, kv_ref, stat_ref, *scratch)
+
+    @pl.when(late != 0)
+    def _():
+        stat_ref[...] = before_ref[...]
 
 
 def far_kernel(
@@ -285,14 +324,14 @@
         store.wait()
 
 
-def attend_own(low, queries, out_grad, key_tensor, value_tensor, after):
+def attend_own(late, before, low, queries, out_grad, pair):
     return call(
         own_kernel,
-        [jax.ShapeDtypeStruct((2, KV_HEADS, 8, GROUP_WIDTH * BLOCK), jnp.float32)],
-        [VMEM] * 5 + [ANY],
-        low, queries, out_grad, key_tensor, value_tensor, after,
-        scratch=[pltpu.VMEM((2, BLOCK, CHUNK * BLOCK), jnp.float32)],
-        limit=24 * MIB,
+        [STAT],
+        [SMEM, VMEM, VMEM, ANY, ANY, VMEM],
+        late, before, low, queries, out_grad, pair,
+        scratch=OWN_SCRATCH,
+        limit=52 * MIB,
     )
 
 
@@ -367,11 +406,15 @@
     low = first.reshape(2, BLOCK) - (start - LIMIT)[:, None]
     low = jnp.tile(low, (1, CHUNK)).reshape(2, 1, CHUNK * BLOCK)
 
+    late = ((grp_index == 1) | ((grp_index % 2 == 0) & (grp_index > 0))).astype(jnp.int32)
+    late = late.reshape(1)
+
+    pair = jnp.stack([key_tensor, value_tensor])
     (packed,) = call(
         pack_kernel,
         [bf16((PIECES, 2, *tile))],
         [VMEM],
-        jnp.stack([key_tensor, value_tensor]),
+        pair,
     )
     place = jnp.clip(placement, 0, SLOTS - 1)
     pieces = exchange(packed).reshape(SLOTS, *tile)
@@ -383,18 +426,17 @@
         pieces,
     )
     prev = lax.ppermute(last, "grp", [(i, i + 1) for i in range(grp_count - 1)])
-    wanted, done = call(
+    wanted, before = call(
         spread_kernel,
-        [bf16((SLOTS, BEFORE, *tile)), jax.ShapeDtypeStruct((8, HEAD), jnp.float32)],
-        [SMEM, VMEM, VMEM],
-        place,
-        ordered,
-        prev,
-        scratch=[pltpu.VMEM((SLOTS + BEFORE, *tile), jnp.bfloat16)],
+        [bf16((SLOTS, BEFORE, *tile)), STAT],
+        [SMEM, SMEM, VMEM, VMEM, VMEM, ANY, ANY, VMEM],
+        late, place, ordered, prev, low, queries, out_grad, pair,
+        scratch=[pltpu.VMEM((SLOTS + BEFORE, *tile), jnp.bfloat16), *OWN_SCRATCH],
+        limit=52 * MIB,
     )
     far = exchange(wanted.reshape(ctx_count, 2, BEFORE, *tile))
     far = far.reshape(2, KV_HEADS, PARTS, 2, BEFORE, *tile)
-    (stat,) = attend_own(low, queries, out_grad, key_tensor, value_tensor, done)
+    (stat,) = attend_own(late, before, low, queries, out_grad, pair)
     far_grad, low = attend_far(low, queries, out_grad, stat, far)
     attended, query_grad, own_k, own_v = attend_rest(
         low, queries, out_grad, key_tensor, value_tensor, far

time: 121 us -> 118 us (0.975)
  waiting for transfers between devices: 42.8 us -> 40 us
  Pallas kernels: 24.5 us -> 27.2 us
  local copies, waits for them, and re-layouts: 2.94 us -> 1.15 us
  starting transfers between devices: 29.5 us -> 28.2 us
    all_to_all x1, waiting for transfers between devices: 10.5 us -> 7.41 us  [body(): pieces = exchange(packed).reshape(SLOTS, *tile)]
    pallas_call x10, Pallas kernels: 24.5 us -> 27.2 us  [call(): pl.pallas_call(kernel, in_specs=specs, out_specs=out_specs or [VMEM] * le...]
    unnamed x14 -> x4, local copies, waits for them, and re-layouts: 2.49 us -> 0.01 us
    all_to_all x1, waiting for transfers between devices: 17.6 us -> 18.8 us  [body(): far = exchange(wanted.reshape(ctx_count, 2, BEFORE, *tile))]
  transfers between devices with their start and end apart: 5 -> 5, of which waited for: 5 -> 5; matrix products, arithmetic and copies ran while one was open for 2% -> 3% of each run, Pallas kernels for 11% -> 10%
where the time goes in v4:
time: 118 us
  waiting for transfers between devices  40 us (34%)
  starting transfers between devices  28.2 us (24%)
  Pallas kernels  27.2 us (23%)
  blocking collectives  16.5 us (14%)
  other arithmetic  3.78 us (3%)
    pallas_call x10, Pallas kernels, call(): pl.pallas_call(kernel, in_specs=specs, out_specs=out_specs or [VMEM] * le...  27.2 us
    all_to_all x1, waiting for transfers between devices, body(): far = exchange(wanted.reshape(ctx_count, 2, BEFORE, *tile))  18.8 us
    all_to_all x1, blocking collectives, body(): sums = exchange(sums.reshape(ctx_count, 2, *tile))  16.5 us
    all_to_all x1, starting transfers between devices, body(): pieces = exchange(packed).reshape(SLOTS, *tile)  12 us
    all_to_all x1, waiting for transfers between devices, body(): parts = exchange(far_grad.reshape(ctx_count, 2, BEFORE, *tile))  10.8 us
    all_to_all x1, waiting for transfers between devices, body(): pieces = exchange(packed).reshape(SLOTS, *tile)  7.41 us
    ppermute x1, starting transfers between devices, body(): prev = lax.ppermute(last, 'grp', [(i, i + 1) for i in range(grp_count - 1)])  5.46 us
    all_to_all x1, starting transfers between devices, body(): parts = exchange(far_grad.reshape(ctx_count, 2, BEFORE, *tile))  4.89 us
  transfers between devices with their start and end apart: 5, of which 5 were waited for; matrix products, arithmetic and copies ran while one was open for 3% of the time, Pallas kernels for 10%

profile of v4, /device:TPU:1, one launch (start us, length us, event | category | flops | bytes accessed | tf_op | source)
XLA Modules:
  0.0 117.6 jit_solution(12905856685574775875)
XLA Ops:
  0.6 1.0 pad_maximum_fusion.rows_ref.kv_ref
  1.6 0.7 shard_map.93
  2.4 12.0 %all-to-all-start = ((bf16[32,2,16,128]{3,2,1,0:T(8,128)(2,1)}), bf16[32,2,16,128]{3,2,1,0:T(8,128)(2,1)S(1)}, u32[]{:S(2)}, u32[]{:S(2)}) async-start(bf16[32,2,16,128]{3,2,1,0:T(8,128)(2,1)} %shard_map.93), calls=%async_computation | async-start | bytes 524288 | tf_op jit(solution)/shard_map/all_to_all | solution.py:420
  14.4 0.7 broadcast_add_fusion
  15.2 0.1 iota_add_fusion
  15.2 0.1 add.42
  15.3 0.7 pad_bitcast_fusion
  16.0 0.3 reduce-window.9
  16.3 0.1 slice.10
  16.4 0.1 slice_reduce_fusion
  16.5 0.1 add_bitcast_fusion
  16.6 0.7 slice_subtract_fusion
  17.3 0.2 select_reduce_fusion
  17.5 0.1 reshape.87
  17.5 0.7 broadcast_clamp_fusion.place_ref
  18.2 7.4 %all-to-all-done = bf16[32,2,16,128]{3,2,1,0:T(8,128)(2,1)S(1)} async-done(((bf16[32,2,16,128]{3,2,1,0:T(8,128)(2,1)}), bf16[32,2,16,128]{3,2,1,0:T(8,128)(2,1)S(1)}, u32[]{:S(2)}, u32[]{:S(2)}) %all-to-all-start) | async-done | bytes 262176 | tf_op jit(solution)/shard_map/all_to_all | solution.py:420
  25.6 0.6 shard_map.94
  26.2 5.5 %collective-permute-start = (bf16[3,16,128]{2,1,0:T(8,128)(2,1)S(1)}, bf16[3,16,128]{2,1,0:T(8,128)(2,1)S(1)}, u32[]{:S(2)}, u32[]{:S(2)}) collective-permute-start(bf16[3,16,128]{2,1,0:T(8,128)(2,1)S(1)} %get-tuple-element.19), channel_id=1, source_target_pairs={{0,32},{32,64},{64,96},{96,128},{128,160},{160,192},{192,224},{1,3... | collective-permute-start | bytes 36872 | tf_op jit(solution)/shard_map/ppermute | solution.py:428
  31.7 0.1 broadcast_subtract_fusion
  31.8 0.1 tile.9.low_ref
  31.8 0.6 collective-permute-done.prev_ref
  32.5 4.9 %shard_map.95 = (bf16[64,3,16,128]{3,2,1,0:T(8,128)(2,1)}, f32[2,4,8,1024]{3,2,1,0:T(8,128)S(1)}) custom-call(s32[1]{0:T(128)} %bitcast.2.late_ref, s32[64]{0:T(128)S(1)} %broadcast_clamp_fusion.place_ref, bf16[64,16,128]{2,1,0:T(8,128)(2,1)S(1)} %get-tuple-element.18.ordered_ref, bf16[3,16,128]{2,1,0:T(8,128)(2,1)S(1)} %collective-permute-done.prev_ref, ...), custom_call_target="tpu_custom_call" | custom-call | tf_op jit(solution)/shard_map/pallas_call | solution.py:377
  37.3 3.9 %all-to-all-start.1 = ((bf16[32,2,3,16,128]{4,3,2,1,0:T(8,128)(2,1)}), bf16[32,2,3,16,128]{4,3,2,1,0:T(8,128)(2,1)S(1)}, u32[]{:S(2)}, u32[]{:S(2)}) async-start(bf16[32,2,3,16,128]{4,3,2,1,0:T(8,128)(2,1)} %bitcast.6), calls=%async_computation.1 | async-start | bytes 1572864 | tf_op jit(solution)/shard_map/all_to_all | solution.py:437
  41.3 0.1 shard_map.96.stat_ref
  41.4 18.8 %all-to-all-done.1 = bf16[32,2,3,16,128]{4,3,2,1,0:T(8,128)(2,1)S(1)} async-done(((bf16[32,2,3,16,128]{4,3,2,1,0:T(8,128)(2,1)}), bf16[32,2,3,16,128]{4,3,2,1,0:T(8,128)(2,1)S(1)}, u32[]{:S(2)}, u32[]{:S(2)}) %all-to-all-start.1) | async-done | bytes 786464 | tf_op jit(solution)/shard_map/all_to_all | solution.py:437
  60.2 0.0 copy-start
  60.2 0.0 copy-start.1
  60.2 7.7 %shard_map.97 = (bf16[2,4,4,2,3,16,128]{6,5,4,3,2,1,0:T(8,128)(2,1)}, s32[2,1,256]{2,1,0:T(1,128)S(1)}) custom-call(s32[2,1,256]{2,1,0:T(1,128)S(1)} %tile.9.low_ref, bf16[128,8192]{1,0:T(8,128)(2,1)} %q_ref.7, bf16[128,8192]{1,0:T(8,128)(2,1)} %g_ref.7, f32[2,4,8,1024]{3,2,1,0:T(8,128)S(1)} %shard_map.96.stat_ref, ...), custom_call_target="tpu_custom_call" | custom-call | tf_op jit(solution)/shard_map/pallas_call | solution.py:377
  67.9 4.9 %all-to-all-start.2 = ((bf16[32,2,3,16,128]{4,3,2,1,0:T(8,128)(2,1)}), bf16[32,2,3,16,128]{4,3,2,1,0:T(8,128)(2,1)S(1)}, u32[]{:S(2)}, u32[]{:S(2)}) async-start(bf16[32,2,3,16,128]{4,3,2,1,0:T(8,128)(2,1)} %bitcast.8), calls=%async_computation.2 | async-start | bytes 1572864 | tf_op jit(solution)/shard_map/all_to_all | solution.py:445
  72.8 0.0 copy-done
  72.8 0.0 copy-done.1
  72.8 10.5 %shard_map.98 = (bf16[128,8192]{1,0:T(8,128)(2,1)}, bf16[128,8192]{1,0:T(8,128)(2,1)}, f32[128,512]{1,0:T(8,128)S(1)}, f32[128,512]{1,0:T(8,128)S(1)}) custom-call(s32[2,1,256]{2,1,0:T(1,128)S(1)} %get-tuple-element.22.low_ref, bf16[128,8192]{1,0:T(8,128)(2,1)} %q_ref.7, bf16[128,8192]{1,0:T(8,128)(2,1)} %g_ref.7, bf16[128,512]{1,0:T(8,128)(2,1)S(1)} %copy-done.1, ...), custom_call_target="tpu_custom_call" | custom-call | tf_op jit(solution)/shard_map/pallas_call | solution.py:377
  83.3 10.8 %all-to-all-done.2 = bf16[32,2,3,16,128]{4,3,2,1,0:T(8,128)(2,1)S(1)} async-done(((bf16[32,2,3,16,128]{4,3,2,1,0:T(8,128)(2,1)}), bf16[32,2,3,16,128]{4,3,2,1,0:T(8,128)(2,1)S(1)}, u32[]{:S(2)}, u32[]{:S(2)}) %all-to-all-start.2) | async-done | bytes 786464 | tf_op jit(solution)/shard_map/all_to_all | solution.py:445
  94.1 0.7 shard_map.100
  94.8 1.9 %collective-permute-start.1 = (bf16[3,16,128]{2,1,0:T(8,128)(2,1)S(1)}, bf16[3,16,128]{2,1,0:T(8,128)(2,1)S(1)}, u32[]{:S(2)}, u32[]{:S(2)}) collective-permute-start(bf16[3,16,128]{2,1,0:T(8,128)(2,1)S(1)} %shard_map.100), channel_id=1, source_target_pairs={{32,0},{64,32},{96,64},{128,96},{160,128},{192,160},{224,192},{33,... | collective-permute-start | bytes 36872 | tf_op jit(solution)/shard_map/ppermute | solution.py:461
  96.7 0.7 shard_map.99
  97.4 2.4 %collective-permute-done.1.next_ref = bf16[3,16,128]{2,1,0:T(8,128)(2,1)S(1)} collective-permute-done((bf16[3,16,128]{2,1,0:T(8,128)(2,1)S(1)}, bf16[3,16,128]{2,1,0:T(8,128)(2,1)S(1)}, u32[]{:S(2)}, u32[]{:S(2)}) %collective-permute-start.1) | collective-permute-done | bytes 12320 | tf_op jit(solution)/shard_map/ppermute | solution.py:461
  99.8 0.6 shard_map.101
  100.4 16.5 %all_to_all.20.pieces_ref = bf16[32,2,16,128]{3,2,1,0:T(8,128)(2,1)S(1)} all-to-all(bf16[32,2,16,128]{3,2,1,0:T(8,128)(2,1)S(1)} %bitcast.17), channel_id=1, replica_groups=mesh['grp'=8,'ctx'=32] {'ctx'}, dimensions={0} | all-to-all | bytes 524288 | tf_op jit(solution)/shard_map/all_to_all | solution.py:480
  116.9 0.7 shard_map.102
  (2 shorter events, 0.0 us)
Async XLA Ops:
  2.4 23.2 %all-to-all-start = ((bf16[32,2,16,128]{3,2,1,0:T(8,128)(2,1)}), bf16[32,2,16,128]{3,2,1,0:T(8,128)(2,1)S(1)}, u32[]{:S(2)}, u32[]{:S(2)}) async-start(bf16[32,2,16,128]{3,2,1,0:T(8,128)(2,1)} %shard_map.93), calls=%async_computation | async-start | bytes 524288 | tf_op jit(solution)/shard_map/all_to_all | solution.py:420
  26.2 6.3 %collective-permute-start = (bf16[3,16,128]{2,1,0:T(8,128)(2,1)S(1)}, bf16[3,16,128]{2,1,0:T(8,128)(2,1)S(1)}, u32[]{:S(2)}, u32[]{:S(2)}) collective-permute-start(bf16[3,16,128]{2,1,0:T(8,128)(2,1)S(1)} %get-tuple-element.19), channel_id=1, source_target_pairs={{0,32},{32,64},{64,96},{96,128},{128,160},{160,192},{192,224},{1,3... | collective-permute-start | bytes 36872 | tf_op jit(solution)/shard_map/ppermute | solution.py:428
  37.3 22.9 %all-to-all-start.1 = ((bf16[32,2,3,16,128]{4,3,2,1,0:T(8,128)(2,1)}), bf16[32,2,3,16,128]{4,3,2,1,0:T(8,128)(2,1)S(1)}, u32[]{:S(2)}, u32[]{:S(2)}) async-start(bf16[32,2,3,16,128]{4,3,2,1,0:T(8,128)(2,1)} %bitcast.6), calls=%async_computation.1 | async-start | bytes 1572864 | tf_op jit(solution)/shard_map/all_to_all | solution.py:437
  60.2 12.6 %copy-start = (bf16[128,512]{1,0:T(8,128)(2,1)S(1)}, bf16[128,512]{1,0:T(8,128)(2,1)}, u32[]{:S(2)}) copy-start(bf16[128,512]{1,0:T(8,128)(2,1)} %v_ref.1) | copy-start | bytes 393220
  60.2 12.6 %copy-start.1 = (bf16[128,512]{1,0:T(8,128)(2,1)S(1)}, bf16[128,512]{1,0:T(8,128)(2,1)}, u32[]{:S(2)}) copy-start(bf16[128,512]{1,0:T(8,128)(2,1)} %k_ref.1) | copy-start | bytes 393220
  67.9 26.2 %all-to-all-start.2 = ((bf16[32,2,3,16,128]{4,3,2,1,0:T(8,128)(2,1)}), bf16[32,2,3,16,128]{4,3,2,1,0:T(8,128)(2,1)S(1)}, u32[]{:S(2)}, u32[]{:S(2)}) async-start(bf16[32,2,3,16,128]{4,3,2,1,0:T(8,128)(2,1)} %bitcast.8), calls=%async_computation.2 | async-start | bytes 1572864 | tf_op jit(solution)/shard_map/all_to_all | solution.py:445
  94.8 5.0 %collective-permute-start.1 = (bf16[3,16,128]{2,1,0:T(8,128)(2,1)S(1)}, bf16[3,16,128]{2,1,0:T(8,128)(2,1)S(1)}, u32[]{:S(2)}, u32[]{:S(2)}) collective-permute-start(bf16[3,16,128]{2,1,0:T(8,128)(2,1)S(1)} %shard_map.100), channel_id=1, source_target_pairs={{32,0},{64,32},{96,64},{128,96},{160,128},{192,160},{224,192},{33,... | collective-permute-start | bytes 36872 | tf_op jit(solution)/shard_map/ppermute | solution.py:461
